TPU v7x, 512 devices: a whole 4x4x16 slice. The times are simulated.
512 devices in a mesh: gx: 16 (over y_hi, x, core), gy: 32 (over z, y_lo).
Axes of the slice: x: 4, y: 4 (y_hi: 2, y_lo: 2; y = y_hi * 2 + y_lo), z: 16, core: 2. Of those that a mesh axis runs over, the one named last changes fastest.
Arguments:
- rel_pos: float32 [3, 10485760], P(None, ('gx', 'gy')), may hold values from -0.5 to 0.5
- charges: float32 [4, 10485760], P(None, ('gx', 'gy')), may hold values from -0.1875 to 0.1875
- block_cell: int32 [81920], P(('gx', 'gy')), may hold values from 0 to 127, as said below
- block_count: int32 [81920], P(('gx', 'gy')), may hold values from 1 to 128, as said below
- leaf_offsets: int32 [96, 3], replicated, may hold values from -3 to 3, as said below
- coarse_offsets: int32 [96, 3], replicated, may hold values from -3 to 3, as said below
- leaf_ops: float32 [96, 25, 25], replicated, may hold values from -0.125 to 0.125
- coarse_ops: float32 [96, 25, 25], replicated, may hold values from -0.125 to 0.125
- upward_ops: float32 [8, 25, 25], replicated, may hold values from -0.4375 to 0.4375
- downward_ops: float32 [8, 25, 25], replicated, may hold values from -1.25 to 1.25
Outputs:
- potential: float32 [4, 10485760], P(None, ('gx', 'gy'))
Inputs may be any that keep to these rules, and one draw needn't show every extreme that they name: `block_cell`: within the 160 blocks of one column the values never fall, and every value 0 to 127 occurs. `block_count`: every block that is not the last block of its leaf cell holds 128 live atoms; the live atoms come first in a block. `leaf_offsets`: the rows are distinct offsets (dx, dy, dz) with |dx| <= 2, |dy| <= 2, |dz| <= 3 and max(|dx|, |dy|, |dz|) >= 2; (2, 0, 0), (-2, 0, 0), (0, 2, 0), (0, -2, 0), (0, 0, 3) and (0, 0, -3) are among them. `coarse_offsets`: the rows are distinct offsets (dx, dy, dz) with |dx| <= 2, |dy| <= 2, |dz| <= 3 and max(|dx|, |dy|, |dz|) >= 2; (2, 0, 0), (-2, 0, 0), (0, 2, 0), (0, -2, 0), (0, 0, 3) and (0, 0, -3) are among them.
All inputs are finite; a program needn't handle non-finite values.
Results may differ from a plain program's by a relative error of at most 0.0003.
Values sent between devices are 32-bit elements; how exact they have to be, the bound alone decides.
No kernel may reach another device: no remote copies, remote signals or barrier semaphores. Data moves between devices by JAX's collectives and lax.ppermute only.
A program may use at most 64 MiB of HBM per device.

v0:
```python
import math

import jax
import jax.numpy as jnp
from jax import lax
from jax.experimental import pallas as pl
from jax.experimental.pallas import tpu as pltpu
from jax.sharding import PartitionSpec as P

NQ = 4
NP = 25
NZ = 128
BLKS = 160
LANES = 256
EXTRA = BLKS - 128
SLOT = 128
CLS = 96
PAD = 32
LEAF = 104
PAIR = 56
GROUP = 48
TILES = 13
DEPTH = TILES * NZ
F32 = jnp.float32
BF16 = jnp.bfloat16

VMEM = pl.BlockSpec(memory_space=pltpu.VMEM)
HBM = pl.BlockSpec(memory_space=pltpu.HBM)


def harmonics(pos_x, pos_y, pos_z):
    point_x = 2.0 * pos_x
    point_y = 2.0 * pos_y
    point_z = 2.0 * pos_z
    radius_sq = point_x * point_x + point_y * point_y + point_z * point_z
    real_part = {(0, 0): jnp.ones_like(point_x)}
    imag_part = {}
    for degree in range(1, 5):
        lower_real = real_part[degree - 1, degree - 1]
        if degree == 1:
            real_part[1, 1] = point_x * 0.5
            imag_part[1, 1] = point_y * 0.5
        else:
            lower_imag = imag_part[degree - 1, degree - 1]
            scale = 1.0 / (2.0 * degree)
            real_part[degree, degree] = (point_x * lower_real - point_y * lower_imag) * scale
            imag_part[degree, degree] = (point_x * lower_imag + point_y * lower_real) * scale
        for azimuth in range(degree):
            scale = 1.0 / float((degree + azimuth) * (degree - azimuth))
            scale_z = ((2.0 * degree - 1.0) * scale) * point_z
            if degree == 1:
                real_part[1, 0] = scale_z
                continue
            next_real = scale_z * real_part[degree - 1, azimuth]
            if degree - 2 >= azimuth:
                scaled_sq = radius_sq * scale
                next_real = next_real - scaled_sq * real_part[degree - 2, azimuth]
            real_part[degree, azimuth] = next_real
            if azimuth > 0:
                next_imag = scale_z * imag_part[degree - 1, azimuth]
                if degree - 2 >= azimuth:
                    next_imag = next_imag - scaled_sq * imag_part[degree - 2, azimuth]
                imag_part[degree, azimuth] = next_imag
    rows_out = []
    for degree in range(5):
        rows_out.append(real_part[degree, 0] * float(math.factorial(degree)))
        for azimuth in range(1, degree + 1):
            factor = math.sqrt(math.factorial(degree + azimuth) * math.factorial(degree - azimuth))
            rows_out.append(real_part[degree, azimuth] * factor)
            rows_out.append(imag_part[degree, azimuth] * factor)
    return rows_out


def split(value):
    high = value.astype(BF16)
    low = (value - high.astype(F32)).astype(BF16)
    return high, low


def dot(left, right):
    return lax.dot_general(left, right, (((1,), (0,)), ((), ())), preferred_element_type=F32)


def exact_dot(left, right):
    return lax.dot_general(
        left,
        right,
        (((1,), (0,)), ((), ())),
        preferred_element_type=F32,
        precision=lax.Precision.HIGHEST,
    )


def unpacked(field, channel, channels):
    zeros = jnp.zeros((PAD - NP, NZ), F32)
    return jnp.concatenate(
        [
            field[channel * 24 : channel * 24 + 24],
            field[channels * 24 + channel : channels * 24 + channel + 1],
            zeros,
        ],
        axis=0,
    )


def store_packed(ref, base, channel, channels, value):
    ref[base + channel * 24 : base + channel * 24 + 24, :] = value[:24]
    row = base + channels * 24 + channel
    ref[row : row + 1, :] = value[24:25]


def even_lanes(shape):
    return lax.broadcasted_iota(jnp.int32, shape, 1) % 2 == 0


def octant_rows(ref, octant):
    return ref.reshape(NP * 8, NP)[pl.ds(octant, NP, stride=8), :]


def parity(axis):
    return lax.rem(lax.axis_index(axis), 2)


def slots_down(tile):
    extra = tile[SLOT:, :]
    runs = [extra[:, g * EXTRA : (g + 1) * EXTRA] for g in range(4)]
    return jnp.concatenate([tile[:SLOT, :].T, jnp.concatenate(runs, axis=0).T], axis=0)


def blocks_down(tile):
    extra = tile[SLOT:, :].T
    runs = [extra[g * EXTRA : (g + 1) * EXTRA, :] for g in range(4)]
    return jnp.concatenate([tile[:SLOT, :].T, jnp.concatenate(runs, axis=1)], axis=0)


def spread_row(values, row):
    row[:, 0:SLOT] = values[:, 0:SLOT]
    for g in range(4):
        row[:, SLOT + g * EXTRA : SLOT + (g + 1) * EXTRA] = values[:, SLOT:BLKS]
    return row[...]


def member_t(cell_ref, row):
    cells = lax.broadcasted_iota(jnp.int32, (NZ, LANES), 0)
    return (cells == spread_row(cell_ref, row)).astype(F32)


def live_t(count_ref, row):
    counts = spread_row(count_ref, row)
    first = lax.broadcasted_iota(jnp.int32, (SLOT, SLOT), 0)
    run = lax.broadcasted_iota(jnp.int32, (EXTRA, SLOT), 1) // EXTRA
    second = lax.broadcasted_iota(jnp.int32, (EXTRA, SLOT), 0) + run * EXTRA
    return jnp.concatenate([first < counts[:, :SLOT], second < counts[:, SLOT:]], axis=0)


def moments_kernel(
    pos_in, charge_in, cell_in, count_in, upward_in, out, *scratch
):
    pos, charge, cell, count, upward, basis, weight, sums, row, ops, done = scratch
    copies = [
        pltpu.make_async_copy(source, target, done.at[n])
        for n, (source, target) in enumerate(
            (
                (pos_in, pos),
                (charge_in, charge),
                (cell_in, cell),
                (count_in, count),
                (upward_in, upward),
            )
        )
    ]
    for copy in copies:
        copy.start()
    copies[0].wait()
    coords = [slots_down(pos[:, d, :]) for d in range(3)]
    for j, value in enumerate(harmonics(*coords)):
        basis[j] = value
    for copy in copies[1:]:
        copy.wait()
    live = live_t(count, row)
    for q in range(NQ):
        weight[q] = jnp.where(live, slots_down(charge[:, q, :]), 0.0)
    sums[NQ * NP :, :] = jnp.zeros((LEAF - NQ * NP, LANES), F32)
    for j in range(NP):
        value = basis[j]
        for q in range(NQ):
            product = (weight[q] * value).reshape(BLKS // 8, 8, SLOT)
            at = q * 24 + j if j < 24 else 96 + q
            sums[at : at + 1, :SLOT] = jnp.sum(
                jnp.sum(product[: SLOT // 8], axis=0), axis=0, keepdims=True
            )
            sums[at : at + 1, SLOT:] = jnp.sum(
                jnp.sum(product[SLOT // 8 :], axis=0), axis=0, keepdims=True
            )
    member = member_t(cell, row).T.astype(BF16)
    high, low = split(sums[...])
    field = dot(high, member) + dot(low, member)
    out[0:LEAF, :] = field
    ops[...] = jnp.zeros_like(ops)
    octant = (parity("gx") * 2 + parity("gy")) * 2
    for c in range(2):
        ops[c * PAD : c * PAD + NP, 0:NP] = octant_rows(upward, octant + c)
    stacked = jnp.concatenate([unpacked(field, q, NQ) for q in range(NQ)], axis=1)
    raised = exact_dot(ops[...], stacked)
    out[LEAF : LEAF + PAIR, :] = jnp.zeros((PAIR, NZ), F32)
    even = even_lanes((PAD, NZ))
    for pair in range(2):
        first, second = [
            [raised[c * PAD : (c + 1) * PAD, q * NZ : (q + 1) * NZ] for c in range(2)]
            for q in (2 * pair, 2 * pair + 1)
        ]
        value = jnp.where(
            even,
            first[0] + pltpu.roll(first[1], NZ - 1, 1),
            pltpu.roll(second[0], 1, 1) + second[1],
        )
        store_packed(out, LEAF, pair, 2, value)


def tables_kernel(leaf_at, coarse_at, leaf_ops, coarse_ops, leaf_out, coarse_out, codes, left):
    toward = (1 - 2 * parity("gx")).astype(F32)
    lane = lax.broadcasted_iota(jnp.int32, (NZ, NZ), 1).astype(F32)
    for at, ops, out, columns in (
        (leaf_at, leaf_ops, leaf_out, 2),
        (coarse_at, coarse_ops, coarse_out, 1),
    ):
        codes[...] = jnp.full((8, NZ), 99.0, F32)
        codes[0:3, 0:CLS] = at[...].astype(F32)
        turned = codes[...].T
        place = (turned[:, 0:1] + 2.0) * 8.0 + 3.0 - turned[:, 2:3]
        ahead = -toward * turned[:, 1:2]
        picks = []
        for half in range(2):
            found = [lane == place + float(half * GROUP + t * 8) for t in range(columns)]
            picks.append(
                jnp.concatenate(
                    [
                        (found[t] & (ahead == float(r))).astype(F32)
                        for t in range(columns)
                        for r in range(3)
                    ],
                    axis=1,
                )
            )
        pick = jnp.concatenate(picks, axis=0).astype(BF16)
        left[...] = jnp.zeros_like(left)
        for i in range(NP):
            row = (i // 2) * PAD
            col = (i % 2) * NZ
            left[row : row + NP, col : col + CLS] = ops[:, i, :]
        blocks = 3 * columns
        for part, value in enumerate(split(left[...])):
            table = dot(value, pick).astype(BF16)
            for tile in range(TILES):
                for block in range(blocks):
                    row = (part * blocks + block) * PAD
                    out[row : row + PAD, tile * NZ : (tile + 1) * NZ] = table[
                        tile * PAD : (tile + 1) * PAD, block * NZ : (block + 1) * NZ
                    ]


def join_kernel(pairs, far, out):
    out[0:LEAF, :] = pairs[0, 0:LEAF, :]
    out[LEAF : 2 * LEAF, :] = pairs[1, 0:LEAF, :]
    out[2 * LEAF : 2 * LEAF + PAIR, :] = pairs[0, LEAF:, :] + pairs[1, LEAF:, :]
    out[2 * LEAF + PAIR :, :] = far[...]


def translate_kernel(near, sides, leaf_k, coarse_k, one_out, two_out, kept, *scratch):
    fields, high, low = scratch
    core = parity("gx")
    for ref in (high, low):
        for tile in range(TILES):
            used = 2 * GROUP if 2 * tile + 1 < NP else GROUP
            ref[tile * NZ + used : (tile + 1) * NZ, :] = jnp.zeros((NZ - used, NQ * NZ), BF16)

    def spread(columns, channels, step):
        for i in range(NP):
            row = (i // 2) * NZ + (i % 2) * GROUP
            for q in range(channels):
                at = q * 24 + i if i < 24 else channels * 24 + q
                for two in range(3):
                    turned = []
                    for column in columns[2 * two : 2 * two + 2]:
                        if column is None:
                            turned.append(jnp.zeros((8, NZ), F32))
                            continue
                        value = jnp.broadcast_to(fields[column, at : at + 1, :], (8, NZ))
                        turned.append(pltpu.roll(value, 0, 1, stride=step, stride_axis=0))
                    top, rest = split(jnp.concatenate(turned, axis=0))
                    base = row + two * 16
                    high[base : base + 16, q * NZ : (q + 1) * NZ] = top
                    low[base : base + 16, q * NZ : (q + 1) * NZ] = rest

    def product(table, height, width):
        both = dot(table[...], high[:, :width])
        return both[:height] + both[height:] + dot(table[0:height, :], low[:, :width])

    def emit(ref, base, value, channels, rows):
        ref[base + channels * 25 : base + rows, :] = jnp.zeros((rows - channels * 25, NZ), F32)
        for q in range(channels):
            store_packed(ref, base, q, channels, value[:, q * NZ : (q + 1) * NZ])

    def back(value, step):
        return pltpu.roll(value, NZ - 3 * step, 1)

    for a in range(2):
        fields[a] = back(sides[0, a * LEAF : (a + 1) * LEAF, :], 1)
        fields[2 + a] = back(near[a, 0:LEAF, :], 1)
        fields[4 + a] = back(sides[1, a * LEAF : (a + 1) * LEAF, :], 1)
    spread(range(6), NQ, 1)
    result = product(leaf_k, 6 * PAD, NQ * NZ)
    blocks = [result[b * PAD : (b + 1) * PAD] for b in range(6)]
    for t in range(2):
        emit(one_out, t * LEAF, blocks[3 * t + 1], NQ, LEAF)
        emit(two_out, t * LEAF, blocks[3 * t + 2], NQ, LEAF)
    emit(kept, 0, jnp.where(core == 0, blocks[0], blocks[3]), NQ, LEAF)

    one, two = 2 * LEAF, 2 * LEAF + PAIR
    fields[0, 0:PAIR, :] = back(sides[0, two:, :], 2)
    fields[1, 0:PAIR, :] = back(sides[0, one:two, :], 2)
    fields[2, 0:PAIR, :] = back(near[0, LEAF:, :] + near[1, LEAF:, :], 2)
    fields[3, 0:PAIR, :] = back(sides[1, one:two, :], 2)
    fields[4, 0:PAIR, :] = back(sides[1, two:, :], 2)
    spread([0, 1, 2, 3, 4, None], 2, 2)
    result = product(coarse_k, 3 * PAD, 2 * NZ)
    blocks = [result[b * PAD : (b + 1) * PAD] for b in range(3)]
    outer = lax.rem(core + parity("gy"), 2) == 1
    emit(kept, LEAF, jnp.where(core == 0, blocks[0], 0.0), 2, PAIR)
    emit(kept, LEAF + PAIR, jnp.where(outer, blocks[2], blocks[1]), 2, PAIR)
    emit(one_out, 2 * LEAF, jnp.where(outer, blocks[1], blocks[0]), 2, PAIR)
    emit(one_out, 2 * LEAF + PAIR, blocks[2], 2, PAIR)
    emit(two_out, 2 * LEAF, blocks[1], 2, PAIR)
    emit(two_out, 2 * LEAF + PAIR, jnp.where(outer, 0.0, blocks[2]), 2, PAIR)


def relay_kernel(kept, one_in, two_in, out):
    relayed = one_in[2 * LEAF + PAIR :, :] + two_in[2 * LEAF + PAIR :, :]
    out[...] = kept[LEAF + PAIR :, :] + relayed


def exchange_kernel(kept, one_in, two_in, three_in, out):
    there = pl.ds(pl.multiple_of((1 - parity("gx")) * LEAF, 8), LEAF)
    out[0:LEAF, :] = one_in[there, :] + two_in[there, :]
    direct = pl.ds(2 * LEAF, PAIR)
    out[LEAF:, :] = kept[LEAF : LEAF + PAIR, :] + (
        one_in[direct, :] + two_in[direct, :] + three_in[...]
    )


def basis_kernel(pos, after, basis):
    del after
    coords = [slots_down(pos[:, d, :]) for d in range(3)]
    for j, value in enumerate(harmonics(*coords)):
        basis[j] = value


def potential_kernel(
    kept, one_in, two_in, last, cell, count, downward, basis, out, row, ops, spread, result
):
    core = parity("gx")
    mine = pl.ds(pl.multiple_of(core * LEAF, 8), LEAF)
    leaf = kept[0:LEAF, :] + one_in[mine, :] + two_in[mine, :] + last[1 - core, 0:LEAF, :]
    coarse = last[0, LEAF:, :] + last[1, LEAF:, :]
    ops[...] = jnp.zeros_like(ops)
    octant = (parity("gx") * 2 + parity("gy")) * 2
    for c in range(2):
        ops[0:NP, c * PAD : c * PAD + NP] = octant_rows(downward, octant + c)
    even = even_lanes((PAD, NZ))
    columns = []
    for q in range(NQ):
        value = unpacked(coarse, q // 2, 2)
        if q % 2 == 0:
            down = [jnp.where(even, value, 0.0), jnp.where(even, 0.0, pltpu.roll(value, 1, 1))]
        else:
            down = [jnp.where(even, pltpu.roll(value, NZ - 1, 1), 0.0), jnp.where(even, 0.0, value)]
        columns.append(jnp.concatenate(down, axis=0))
    pushed = exact_dot(ops[0:PAD, :], jnp.concatenate(columns, axis=1))
    local = jnp.concatenate(
        [unpacked(leaf, q, NQ) + pushed[:, q * NZ : (q + 1) * NZ] for q in range(NQ)], axis=0
    )
    member = member_t(cell, row).astype(BF16)
    high, low = split(local)
    spread[...] = dot(high, member) + dot(low, member)
    live = live_t(count, row)
    for start, size, lane in ((0, 64, 0), (64, 64, 0), (SLOT, EXTRA, SLOT)):
        totals = [None] * NQ
        for j in range(NP):
            value = basis[j, start : start + size, :]
            for q in range(NQ):
                term = spread[q * PAD + j : q * PAD + j + 1, lane : lane + SLOT] * value
                totals[q] = term if j == 0 else totals[q] + term
        for q in range(NQ):
            result[q, start : start + size, :] = totals[q]
    for q in range(NQ):
        out[:, q, :] = blocks_down(jnp.where(live, result[q], 0.0))


def call(kernel, outs, scratch, specs, name, micros=1, megabytes=24.0):
    return pl.pallas_call(
        kernel,
        out_shape=outs if len(outs) > 1 else outs[0],
        in_specs=specs,
        out_specs=[VMEM] * len(outs) if len(outs) > 1 else VMEM,
        scratch_shapes=scratch,
        cost_estimate=pl.CostEstimate(
            flops=int(micros * 1e9), bytes_accessed=1000000, transcendentals=0
        ),
        compiler_params=pltpu.CompilerParams(vmem_limit_bytes=int(megabytes * 1024 * 1024)),
        name=name,
    )


def rows(count):
    return jax.ShapeDtypeStruct((count, NZ), F32)


def chip_pairs():
    return [[i, i + 1] for i in range(0, lax.axis_size("gx"), 2)]


def outward_x(distance):
    peers = lax.axis_size("gx")
    return [(i, (i + distance if i % 2 else i - distance) % peers) for i in range(peers)]


def along_y(field, distance):
    wide, tall = lax.axis_size("gx"), lax.axis_size("gy")
    route = []
    for x in range(wide):
        step = -distance if x % 2 else distance
        route += [(x * tall + y, x * tall + (y + step) % tall) for y in range(tall)]
    return lax.ppermute(field, ("gx", "gy"), route)


def per_device(
    rel_pos,
    charges,
    block_cell,
    block_count,
    leaf_offsets,
    coarse_offsets,
    leaf_ops,
    coarse_ops,
    upward_ops,
    downward_ops,
):
    pos = rel_pos.reshape(3, BLKS, SLOT).transpose(1, 0, 2)
    charge = charges.reshape(NQ, BLKS, SLOT).transpose(1, 0, 2)
    cell = block_cell.reshape(1, BLKS)
    count = block_count.reshape(1, BLKS)
    upward = upward_ops.transpose(1, 0, 2)
    downward = downward_ops.transpose(1, 0, 2)
    index_row = pltpu.VMEM((1, LANES), jnp.int32)

    own_field = call(
        moments_kernel,
        [rows(LEAF + PAIR)],
        [
            pltpu.VMEM((BLKS, 3, SLOT), F32),
            pltpu.VMEM((BLKS, NQ, SLOT), F32),
            pltpu.VMEM((1, BLKS), jnp.int32),
            pltpu.VMEM((1, BLKS), jnp.int32),
            pltpu.VMEM((NP, 8, NP), F32),
            pltpu.VMEM((NP, BLKS, SLOT), F32),
            pltpu.VMEM((NQ, BLKS, SLOT), F32),
            pltpu.VMEM((LEAF, LANES), F32),
            index_row,
            pltpu.VMEM((2 * PAD, PAD), F32),
            pltpu.SemaphoreType.DMA((5,)),
        ],
        [HBM] * 5,
        "moments",
        3,
        63.9,
    )(pos, charge, cell, count, upward)

    near = lax.all_gather(own_field, "gx", axis_index_groups=chip_pairs())
    beside = lax.ppermute(near, "gx", outward_x(1))
    parents = near[0, LEAF:] + near[1, LEAF:]
    beyond = lax.ppermute(parents, "gx", outward_x(3))
    leaf_k, coarse_k = call(
        tables_kernel,
        [
            jax.ShapeDtypeStruct((12 * PAD, DEPTH), BF16),
            jax.ShapeDtypeStruct((6 * PAD, DEPTH), BF16),
        ],
        [pltpu.VMEM((8, NZ), F32), pltpu.VMEM((TILES * PAD, 2 * NZ), F32)],
        [VMEM] * 4,
        "tables",
        2,
    )(
        leaf_offsets.T,
        coarse_offsets.T,
        leaf_ops.transpose(1, 2, 0),
        coarse_ops.transpose(1, 2, 0),
    )
    side = call(join_kernel, [rows(2 * LEAF + 2 * PAIR)], [], [VMEM] * 2, "join")(beside, beyond)
    sides = lax.all_gather(side, "gx", axis_index_groups=chip_pairs())

    one, two, kept = call(
        translate_kernel,
        [rows(2 * LEAF + 2 * PAIR), rows(2 * LEAF + 2 * PAIR), rows(LEAF + 2 * PAIR)],
        [pltpu.VMEM((6, LEAF, NZ), F32)] + [pltpu.VMEM((DEPTH, NQ * NZ), BF16)] * 2,
        [VMEM] * 4,
        "translate",
        3,
    )(near, sides, leaf_k, coarse_k)

    one = along_y(one, 1)
    two = along_y(two, 2)
    relayed = call(relay_kernel, [rows(PAIR)], [], [VMEM] * 3, "relay")(kept, one, two)
    three = along_y(relayed, 3)
    basis = call(
        basis_kernel,
        [jax.ShapeDtypeStruct((NP, BLKS, SLOT), F32)],
        [],
        [VMEM] * 2,
        "basis",
    )(pos, kept)
    passed = call(exchange_kernel, [rows(LEAF + PAIR)], [], [VMEM] * 4, "exchange")(
        kept, one, two, three
    )
    last = lax.all_gather(passed, "gx", axis_index_groups=chip_pairs())

    potential = call(
        potential_kernel,
        [jax.ShapeDtypeStruct((BLKS, NQ, SLOT), F32)],
        [
            index_row,
            pltpu.VMEM((PAD, 2 * PAD), F32),
            pltpu.VMEM((NQ * PAD, LANES), F32),
            pltpu.VMEM((NQ, BLKS, SLOT), F32),
        ],
        [VMEM] * 8,
        "potential",
        3,
    )(kept, one, two, last, cell, count, downward, basis)
    return potential.transpose(1, 0, 2).reshape(NQ, BLKS * SLOT)


def solution(mesh):
    in_specs = (
        P(None, ("gx", "gy")),
        P(None, ("gx", "gy")),
        P(("gx", "gy")),
        P(("gx", "gy")),
        P(),
        P(),
        P(),
        P(),
        P(),
        P(),
    )
    out_specs = P(None, ("gx", "gy"))
    return jax.shard_map(
        per_device, mesh=mesh, in_specs=in_specs, out_specs=out_specs, check_vma=False
    )
```

profile of v0, /device:TPU:1, one launch (start us, length us, event | category | flops | bytes accessed | tf_op | source)
XLA Modules:
  0.0 58.2 jit_solution(18282488844608524186)
XLA Ops:
  0.0 0.0 copy-start.4
  0.0 0.0 copy-start.5
  0.0 3.6 %moments.1 = f32[160,128]{1,0:T(8,128)} custom-call(f32[160,3,128]{2,1,0:T(4,128)} %bitcast.29, f32[160,4,128]{2,1,0:T(4,128)} %bitcast.38, s32[1,160]{1,0:T(1,128)} %bitcast.34, s32[1,160]{1,0:T(1,128)} %bitcast.36, f32[25,8,25]{2,1,0:T(8,128)} %bitcast.39), custom_call_target="tpu_custom_call" | custom-call | flops 3000000000 | bytes 1000000 | tf_op jit(solution)/shard_map/moments/pallas_call | solution.py:456
  3.6 8.7 %all-gather = f32[320,128]{1,0:T(8,128)S(1)} all-gather(f32[160,128]{1,0:T(8,128)} %moments.1), channel_id=2, replica_groups={{0,32},{64,96},{128,160},{192,224},{256,288},{320,352},{384,416},{448,4..., dimensions={0}, use_global_device_ids=true | all-gather | bytes 245760 | tf_op jit(solution)/shard_map/all_gather | solution.py:478
  12.3 1.9 %collective-permute-start = (f32[2,160,128]{2,1,0:T(8,128)S(1)}, f32[2,160,128]{2,1,0:T(8,128)S(1)}, u32[]{:S(2)}, u32[]{:S(2)}) collective-permute-start(f32[2,160,128]{2,1,0:T(8,128)S(1)} %bitcast.23), channel_id=1, source_target_pairs={{0,480},{32,64},{64,32},{96,128},{128,96},{160,192},{192,160},{224... | collective-permute-start | bytes 491528 | tf_op jit(solution)/shard_map/ppermute | solution.py:479
  14.2 1.9 %collective-permute-start.1 = (f32[56,128]{1,0:T(8,128)S(1)}, f32[56,128]{1,0:T(8,128)S(1)}, u32[]{:S(2)}, u32[]{:S(2)}) collective-permute-start(f32[56,128]{1,0:T(8,128)S(1)} %fusion), channel_id=1, source_target_pairs={{0,416},{32,128},{64,480},{96,192},{128,32},{160,256},{192,96},{22... | collective-permute-start | bytes 86024 | tf_op jit(solution)/shard_map/ppermute | solution.py:481
  16.2 0.0 copy-done.4
  16.2 0.0 copy-done.5
  16.2 0.0 copy-start
  16.2 1.0 %copy-done = f32[96,25,25]{0,2,1:T(8,128)S(1)} copy-done((f32[96,25,25]{0,2,1:T(8,128)S(1)}, f32[96,25,25]{0,2,1:T(8,128)}, u32[]{:S(2)}) %copy-start) | copy-done | bytes 240024
  17.2 0.0 copy-start.1
  17.2 1.0 %copy-done.1 = f32[96,25,25]{0,2,1:T(8,128)S(1)} copy-done((f32[96,25,25]{0,2,1:T(8,128)S(1)}, f32[96,25,25]{0,2,1:T(8,128)}, u32[]{:S(2)}) %copy-start.1) | copy-done | bytes 240024
  18.2 1.4 %tables.1 = (bf16[384,1664]{1,0:T(8,128)(2,1)S(1)}, bf16[192,1664]{1,0:T(8,128)(2,1)S(1)}) custom-call(s32[3,96]{1,0:T(4,128)S(1)} %bitcast.32, s32[3,96]{1,0:T(4,128)S(1)} %bitcast.33, f32[25,25,96]{2,1,0:T(8,128)S(1)} %bitcast.27, f32[25,25,96]{2,1,0:T(8,128)S(1)} %bitcast.28), custom_call_target="tpu_custom_call" | custom-call | flops 2000000000 | bytes 1000000 | tf_op jit(solution)/shard_map/tables/pallas_call | solution.py:482
  19.6 1.6 %collective-permute-done.1.far = f32[56,128]{1,0:T(8,128)S(1)} collective-permute-done((f32[56,128]{1,0:T(8,128)S(1)}, f32[56,128]{1,0:T(8,128)S(1)}, u32[]{:S(2)}, u32[]{:S(2)}) %collective-permute-start.1) | collective-permute-done | bytes 28704 | tf_op jit(solution)/shard_map/ppermute | solution.py:481
  21.2 0.0 collective-permute-done.pairs
  21.2 4.1 %all-gather.1 = f32[640,128]{1,0:T(8,128)S(1)} all-gather(f32[320,128]{1,0:T(8,128)S(1)} %join.1), channel_id=3, replica_groups={{0,32},{64,96},{128,160},{192,224},{256,288},{320,352},{384,416},{448,4..., dimensions={0}, use_global_device_ids=true | all-gather | bytes 491520 | tf_op jit(solution)/shard_map/all_gather | solution.py:499
  25.4 2.4 %translate.1 = (f32[320,128]{1,0:T(8,128)S(1)}, f32[320,128]{1,0:T(8,128)S(1)}, f32[216,128]{1,0:T(8,128)S(1)}) custom-call(f32[2,160,128]{2,1,0:T(8,128)S(1)} %bitcast.25, f32[2,320,128]{2,1,0:T(8,128)S(1)} %bitcast.22, bf16[384,1664]{1,0:T(8,128)(2,1)S(1)} %get-tuple-element.10.leaf_k, bf16[192,1664]{1,0:T(8,128)(2,1)S(1)} %get-tuple-element.11.coarse_k), custom_call_target="tpu_custom_call" | custom-call | flops 3000000000 | bytes 1000000 | tf_op jit(solution)/shard_map/translate/pallas_call | solution.py:501
  27.8 0.0 copy-start.2
  27.9 11.1 %collective-permute-start.2 = (f32[320,128]{1,0:T(8,128)S(1)}, f32[320,128]{1,0:T(8,128)S(1)}, u32[]{:S(2)}, u32[]{:S(2)}) collective-permute-start(f32[320,128]{1,0:T(8,128)S(1)} %get-tuple-element.13), channel_id=1, source_target_pairs={{0,1},{1,2},{2,3},{3,4},{4,5},{5,6},{6,7},{7,8},{8,9},{9,10},{10,1... | collective-permute-start | bytes 491528 | tf_op jit(solution)/shard_map/ppermute | solution.py:433
  39.0 2.6 %collective-permute-start.3 = (f32[320,128]{1,0:T(8,128)S(1)}, f32[320,128]{1,0:T(8,128)S(1)}, u32[]{:S(2)}, u32[]{:S(2)}) collective-permute-start(f32[320,128]{1,0:T(8,128)S(1)} %get-tuple-element.14), channel_id=1, source_target_pairs={{0,2},{1,3},{2,4},{3,5},{4,6},{5,7},{6,8},{7,9},{8,10},{9,11},{10,... | collective-permute-start | bytes 491528 | tf_op jit(solution)/shard_map/ppermute | solution.py:433
  41.6 0.0 collective-permute-done.2.one_in
  41.7 3.4 %collective-permute-done.3.two_in = f32[320,128]{1,0:T(8,128)S(1)} collective-permute-done((f32[320,128]{1,0:T(8,128)S(1)}, f32[320,128]{1,0:T(8,128)S(1)}, u32[]{:S(2)}, u32[]{:S(2)}) %collective-permute-start.3) | collective-permute-done | bytes 163872 | tf_op jit(solution)/shard_map/ppermute | solution.py:433
  45.1 3.7 %collective-permute-start.4 = (f32[56,128]{1,0:T(8,128)S(1)}, f32[56,128]{1,0:T(8,128)S(1)}, u32[]{:S(2)}, u32[]{:S(2)}) collective-permute-start(f32[56,128]{1,0:T(8,128)S(1)} %relay.1), channel_id=1, source_target_pairs={{0,3},{1,4},{2,5},{3,6},{4,7},{5,8},{6,9},{7,10},{8,11},{9,12},{10... | collective-permute-start | bytes 86024 | tf_op jit(solution)/shard_map/ppermute | solution.py:433
  48.8 0.0 copy-done.2
  48.8 0.5 basis.1
  49.3 0.0 copy-start.3
  49.3 0.0 copy-start.6
  49.3 0.0 copy-start.7
  49.4 1.2 %collective-permute-done.4.three_in = f32[56,128]{1,0:T(8,128)S(1)} collective-permute-done((f32[56,128]{1,0:T(8,128)S(1)}, f32[56,128]{1,0:T(8,128)S(1)}, u32[]{:S(2)}, u32[]{:S(2)}) %collective-permute-start.4) | collective-permute-done | bytes 28704 | tf_op jit(solution)/shard_map/ppermute | solution.py:433
  50.6 5.2 %all-gather.2 = f32[320,128]{1,0:T(8,128)S(1)} all-gather(f32[160,128]{1,0:T(8,128)S(1)} %exchange.1), channel_id=4, replica_groups={{0,32},{64,96},{128,160},{192,224},{256,288},{320,352},{384,416},{448,4..., dimensions={0}, use_global_device_ids=true | all-gather | bytes 245760 | tf_op jit(solution)/shard_map/all_gather | solution.py:524
  55.8 0.0 copy-done.3
  55.8 0.0 copy-done.6
  55.8 0.0 copy-done.7
  55.8 2.4 %potential.1 = f32[160,4,128]{2,1,0:T(4,128)} custom-call(f32[216,128]{1,0:T(8,128)S(1)} %get-tuple-element.12.kept.after, f32[320,128]{1,0:T(8,128)S(1)} %collective-permute-done.2.one_in, f32[320,128]{1,0:T(8,128)S(1)} %collective-permute-done.3.two_in, f32[2,160,128]{2,1,0:T(8,128)S(1)} %bitcast.26, s32[1,160]{1,0:T(1,128)S(1)} %bitcast.35, ...), custom_call_target="tpu_custom_call" | custom-call | flops 3000000000 | bytes 1000000 | tf_op jit(solution)/shard_map/potential/pallas_call | solution.py:526
  (4 shorter events, 0.0 us)
Async XLA Ops:
  0.0 16.2 %copy-start.4 = (s32[96,3]{0,1:T(4,128)S(1)}, s32[96,3]{0,1:T(4,128)}, u32[]{:S(2)}) copy-start(s32[96,3]{0,1:T(4,128)} %param.14) | copy-start | bytes 3460
  0.0 16.2 %copy-start.5 = (s32[96,3]{0,1:T(4,128)S(1)}, s32[96,3]{0,1:T(4,128)}, u32[]{:S(2)}) copy-start(s32[96,3]{0,1:T(4,128)} %param.15) | copy-start | bytes 3460
  12.3 8.9 %collective-permute-start = (f32[2,160,128]{2,1,0:T(8,128)S(1)}, f32[2,160,128]{2,1,0:T(8,128)S(1)}, u32[]{:S(2)}, u32[]{:S(2)}) collective-permute-start(f32[2,160,128]{2,1,0:T(8,128)S(1)} %bitcast.23), channel_id=1, source_target_pairs={{0,480},{32,64},{64,32},{96,128},{128,96},{160,192},{192,160},{224... | collective-permute-start | bytes 491528 | tf_op jit(solution)/shard_map/ppermute | solution.py:479
  14.2 7.0 %collective-permute-start.1 = (f32[56,128]{1,0:T(8,128)S(1)}, f32[56,128]{1,0:T(8,128)S(1)}, u32[]{:S(2)}, u32[]{:S(2)}) collective-permute-start(f32[56,128]{1,0:T(8,128)S(1)} %fusion), channel_id=1, source_target_pairs={{0,416},{32,128},{64,480},{96,192},{128,32},{160,256},{192,96},{22... | collective-permute-start | bytes 86024 | tf_op jit(solution)/shard_map/ppermute | solution.py:481
  16.2 1.0 %copy-start = (f32[96,25,25]{0,2,1:T(8,128)S(1)}, f32[96,25,25]{0,2,1:T(8,128)}, u32[]{:S(2)}) copy-start(f32[96,25,25]{0,2,1:T(8,128)} %param.16) | copy-start | bytes 720004
  17.2 1.0 %copy-start.1 = (f32[96,25,25]{0,2,1:T(8,128)S(1)}, f32[96,25,25]{0,2,1:T(8,128)}, u32[]{:S(2)}) copy-start(f32[96,25,25]{0,2,1:T(8,128)} %param.17) | copy-start | bytes 720004
  27.8 20.9 %copy-start.2 = (f32[3,20480]{1,0:T(4,128)S(1)}, f32[3,20480]{1,0:T(4,128)}, u32[]{:S(2)}) copy-start(f32[3,20480]{1,0:T(4,128)} %param.10) | copy-start | bytes 737284
  27.9 13.8 %collective-permute-start.2 = (f32[320,128]{1,0:T(8,128)S(1)}, f32[320,128]{1,0:T(8,128)S(1)}, u32[]{:S(2)}, u32[]{:S(2)}) collective-permute-start(f32[320,128]{1,0:T(8,128)S(1)} %get-tuple-element.13), channel_id=1, source_target_pairs={{0,1},{1,2},{2,3},{3,4},{4,5},{5,6},{6,7},{7,8},{8,9},{9,10},{10,1... | collective-permute-start | bytes 491528 | tf_op jit(solution)/shard_map/ppermute | solution.py:433
  39.0 6.1 %collective-permute-start.3 = (f32[320,128]{1,0:T(8,128)S(1)}, f32[320,128]{1,0:T(8,128)S(1)}, u32[]{:S(2)}, u32[]{:S(2)}) collective-permute-start(f32[320,128]{1,0:T(8,128)S(1)} %get-tuple-element.14), channel_id=1, source_target_pairs={{0,2},{1,3},{2,4},{3,5},{4,6},{5,7},{6,8},{7,9},{8,10},{9,11},{10,... | collective-permute-start | bytes 491528 | tf_op jit(solution)/shard_map/ppermute | solution.py:433
  45.1 5.5 %collective-permute-start.4 = (f32[56,128]{1,0:T(8,128)S(1)}, f32[56,128]{1,0:T(8,128)S(1)}, u32[]{:S(2)}, u32[]{:S(2)}) collective-permute-start(f32[56,128]{1,0:T(8,128)S(1)} %relay.1), channel_id=1, source_target_pairs={{0,3},{1,4},{2,5},{3,6},{4,7},{5,8},{6,9},{7,10},{8,11},{9,12},{10... | collective-permute-start | bytes 86024 | tf_op jit(solution)/shard_map/ppermute | solution.py:433
  49.3 6.5 %copy-start.3 = (f32[8,25,25]{2,0,1:T(8,128)S(1)}, f32[8,25,25]{2,0,1:T(8,128)}, u32[]{:S(2)}) copy-start(f32[8,25,25]{2,0,1:T(8,128)} %param.19) | copy-start | bytes 60004
  49.3 6.5 %copy-start.6 = (s32[160]{0:T(256)S(1)}, s32[160]{0:T(256)}, u32[]{:S(2)}) copy-start(s32[160]{0:T(256)} %param.12) | copy-start | bytes 1924
  49.3 6.5 %copy-start.7 = (s32[160]{0:T(256)S(1)}, s32[160]{0:T(256)}, u32[]{:S(2)}) copy-start(s32[160]{0:T(256)} %param.13) | copy-start | bytes 1924
where the time goes:
time: 58.6 us; the launch traced here: 58.2 us
  starting transfers between devices  21.3 us (36%)
  blocking collectives  18 us (31%)
  Pallas kernels  10.5 us (18%)
  waiting for transfers between devices  6.22 us (11%)
  local copies, waits for them, and re-layouts  2.03 us (3%)
    ppermute x3, starting transfers between devices, along_y(): return lax.ppermute(field, ('gx', 'gy'), route)  17.5 us
    all_gather x1, blocking collectives, per_device(): near = lax.all_gather(own_field, 'gx', axis_index_groups=chip_pairs())  8.66 us
    all_gather x1, blocking collectives, per_device(): last = lax.all_gather(passed, 'gx', axis_index_groups=chip_pairs())  5.19 us
    ppermute x3, waiting for transfers between devices, along_y(): return lax.ppermute(field, ('gx', 'gy'), route)  4.63 us
    all_gather x1, blocking collectives, per_device(): sides = lax.all_gather(side, 'gx', axis_index_groups=chip_pairs())  4.14 us
    pallas_call x1, Pallas kernels, per_device(): call(moments_kernel, [rows(LEAF + PAIR)], [pltpu.VMEM((BLKS, 3, SLOT), F3...  3.64 us
    pallas_call x1, Pallas kernels, per_device(): call(translate_kernel, [rows(2 * LEAF + 2 * PAIR), rows(2 * LEAF + 2 * PA...  2.45 us
    pallas_call x1, Pallas kernels, per_device(): call(potential_kernel, [jax.ShapeDtypeStruct((BLKS, NQ, SLOT), F32)], [in...  2.45 us
  transfers between devices with their start and end apart: 5, of which 3 were waited for; matrix products, arithmetic and copies ran while one was open for 0% of the time, Pallas kernels for 3%

commit v1 on v0

--- a/solution.py
+++ b/solution.py
@@ -82,13 +82,10 @@
 
 
 def exact_dot(left, right):
-    return lax.dot_general(
-        left,
-        right,
-        (((1,), (0,)), ((), ())),
-        preferred_element_type=F32,
-        precision=lax.Precision.HIGHEST,
-    )
+    high, low = split(left)
+    top, rest = split(right)
+    both = dot(jnp.concatenate([high, low], axis=0), top)
+    return both[: left.shape[0]] + both[left.shape[0] :] + dot(high, rest)
 
 
 def unpacked(field, channel, channels):
@@ -224,6 +221,7 @@
         (leaf_at, leaf_ops, leaf_out, 2),
         (coarse_at, coarse_ops, coarse_out, 1),
     ):
+        reaches = (0, 1, 2) if columns == 2 else (0, 1, 2, -1, -2)
         codes[...] = jnp.full((8, NZ), 99.0, F32)
         codes[0:3, 0:CLS] = at[...].astype(F32)
         turned = codes[...].T
@@ -237,7 +235,7 @@
                     [
                         (found[t] & (ahead == float(r))).astype(F32)
                         for t in range(columns)
-                        for r in range(3)
+                        for r in reaches
                     ],
                     axis=1,
                 )
@@ -248,7 +246,7 @@
             row = (i // 2) * PAD
             col = (i % 2) * NZ
             left[row : row + NP, col : col + CLS] = ops[:, i, :]
-        blocks = 3 * columns
+        blocks = columns * len(reaches)
         for part, value in enumerate(split(left[...])):
             table = dot(value, pick).astype(BF16)
             for tile in range(TILES):
@@ -259,75 +257,90 @@
                     ]
 
 
-def join_kernel(pairs, far, out):
-    out[0:LEAF, :] = pairs[0, 0:LEAF, :]
-    out[LEAF : 2 * LEAF, :] = pairs[1, 0:LEAF, :]
-    out[2 * LEAF : 2 * LEAF + PAIR, :] = pairs[0, LEAF:, :] + pairs[1, LEAF:, :]
+def pair_kernel(near, fields, parents):
+    fields[0:LEAF, :] = near[0, 0:LEAF, :]
+    fields[LEAF : 2 * LEAF, :] = near[1, 0:LEAF, :]
+    total = near[0, LEAF:, :] + near[1, LEAF:, :]
+    fields[2 * LEAF :, :] = total
+    parents[...] = total
+
+
+def join_kernel(fields, far, out):
+    out[0 : 2 * LEAF + PAIR, :] = fields[...]
     out[2 * LEAF + PAIR :, :] = far[...]
 
 
 def translate_kernel(near, sides, leaf_k, coarse_k, one_out, two_out, kept, *scratch):
-    fields, high, low = scratch
+    fields, parents, high, low, coarse_high, coarse_low = scratch
     core = parity("gx")
-    for ref in (high, low):
+    for ref in (high, low, coarse_high, coarse_low):
         for tile in range(TILES):
             used = 2 * GROUP if 2 * tile + 1 < NP else GROUP
-            ref[tile * NZ + used : (tile + 1) * NZ, :] = jnp.zeros((NZ - used, NQ * NZ), BF16)
-
-    def spread(columns, channels, step):
+            ref[tile * NZ + used : (tile + 1) * NZ, :] = jnp.zeros(
+                (NZ - used, ref.shape[1]), BF16
+            )
+
+    def spread(source, columns, high, low, step):
+        channels = high.shape[1] // NZ
+
+        def turned(part, column, at):
+            if column is None:
+                return jnp.zeros((8, NZ), F32)
+            value = jnp.broadcast_to(source[part, column, at : at + 1, :], (8, NZ))
+            return pltpu.roll(value, 0, 1, stride=step, stride_axis=0)
+
         for i in range(NP):
             row = (i // 2) * NZ + (i % 2) * GROUP
             for q in range(channels):
                 at = q * 24 + i if i < 24 else channels * 24 + q
                 for two in range(3):
-                    turned = []
-                    for column in columns[2 * two : 2 * two + 2]:
-                        if column is None:
-                            turned.append(jnp.zeros((8, NZ), F32))
-                            continue
-                        value = jnp.broadcast_to(fields[column, at : at + 1, :], (8, NZ))
-                        turned.append(pltpu.roll(value, 0, 1, stride=step, stride_axis=0))
-                    top, rest = split(jnp.concatenate(turned, axis=0))
                     base = row + two * 16
-                    high[base : base + 16, q * NZ : (q + 1) * NZ] = top
-                    low[base : base + 16, q * NZ : (q + 1) * NZ] = rest
-
-    def product(table, height, width):
-        both = dot(table[...], high[:, :width])
-        return both[:height] + both[height:] + dot(table[0:height, :], low[:, :width])
+                    for part, ref in enumerate((high, low)):
+                        value = jnp.concatenate(
+                            [turned(part, column, at) for column in columns[2 * two : 2 * two + 2]],
+                            axis=0,
+                        )
+                        ref[base : base + 16, q * NZ : (q + 1) * NZ] = value.astype(BF16)
+
+    def product(table, height, high, low):
+        both = dot(table[...], high[...])
+        return both[:height] + both[height:] + dot(table[0:height, :], low[...])
 
     def emit(ref, base, value, channels, rows):
         ref[base + channels * 25 : base + rows, :] = jnp.zeros((rows - channels * 25, NZ), F32)
         for q in range(channels):
             store_packed(ref, base, q, channels, value[:, q * NZ : (q + 1) * NZ])
 
-    def back(value, step):
-        return pltpu.roll(value, NZ - 3 * step, 1)
-
+    def back(target, column, value, step):
+        value = pltpu.roll(value, NZ - 3 * step, 1)
+        top = value.astype(BF16).astype(F32)
+        target[0, column] = top
+        target[1, column] = value - top
+
+    one, two = 2 * LEAF, 2 * LEAF + PAIR
+    back(parents, 0, sides[0, two:, :], 2)
+    back(parents, 1, sides[0, one:two, :], 2)
+    back(parents, 2, near[one:, :], 2)
+    back(parents, 3, sides[1, one:two, :], 2)
+    back(parents, 4, sides[1, two:, :], 2)
     for a in range(2):
-        fields[a] = back(sides[0, a * LEAF : (a + 1) * LEAF, :], 1)
-        fields[2 + a] = back(near[a, 0:LEAF, :], 1)
-        fields[4 + a] = back(sides[1, a * LEAF : (a + 1) * LEAF, :], 1)
-    spread(range(6), NQ, 1)
-    result = product(leaf_k, 6 * PAD, NQ * NZ)
+        back(fields, a, sides[0, a * LEAF : (a + 1) * LEAF, :], 1)
+        back(fields, 2 + a, near[a * LEAF : (a + 1) * LEAF, :], 1)
+        back(fields, 4 + a, sides[1, a * LEAF : (a + 1) * LEAF, :], 1)
+    spread(parents, [0, 1, 2, 3, 4, None], coarse_high, coarse_low, 2)
+    spread(fields, range(6), high, low, 1)
+    result = product(coarse_k, 5 * PAD, coarse_high, coarse_low)
+    coarse = [result[b * PAD : (b + 1) * PAD] for b in range(5)]
+    result = product(leaf_k, 6 * PAD, high, low)
     blocks = [result[b * PAD : (b + 1) * PAD] for b in range(6)]
     for t in range(2):
         emit(one_out, t * LEAF, blocks[3 * t + 1], NQ, LEAF)
         emit(two_out, t * LEAF, blocks[3 * t + 2], NQ, LEAF)
     emit(kept, 0, jnp.where(core == 0, blocks[0], blocks[3]), NQ, LEAF)
-
-    one, two = 2 * LEAF, 2 * LEAF + PAIR
-    fields[0, 0:PAIR, :] = back(sides[0, two:, :], 2)
-    fields[1, 0:PAIR, :] = back(sides[0, one:two, :], 2)
-    fields[2, 0:PAIR, :] = back(near[0, LEAF:, :] + near[1, LEAF:, :], 2)
-    fields[3, 0:PAIR, :] = back(sides[1, one:two, :], 2)
-    fields[4, 0:PAIR, :] = back(sides[1, two:, :], 2)
-    spread([0, 1, 2, 3, 4, None], 2, 2)
-    result = product(coarse_k, 3 * PAD, 2 * NZ)
-    blocks = [result[b * PAD : (b + 1) * PAD] for b in range(3)]
+    blocks = coarse
     outer = lax.rem(core + parity("gy"), 2) == 1
     emit(kept, LEAF, jnp.where(core == 0, blocks[0], 0.0), 2, PAIR)
-    emit(kept, LEAF + PAIR, jnp.where(outer, blocks[2], blocks[1]), 2, PAIR)
+    emit(kept, LEAF + PAIR, jnp.where(outer, blocks[3], blocks[4]), 2, PAIR)
     emit(one_out, 2 * LEAF, jnp.where(outer, blocks[1], blocks[0]), 2, PAIR)
     emit(one_out, 2 * LEAF + PAIR, blocks[2], 2, PAIR)
     emit(two_out, 2 * LEAF, blocks[1], 2, PAIR)
@@ -344,7 +357,7 @@
     out[0:LEAF, :] = one_in[there, :] + two_in[there, :]
     direct = pl.ds(2 * LEAF, PAIR)
     out[LEAF:, :] = kept[LEAF : LEAF + PAIR, :] + (
-        one_in[direct, :] + two_in[direct, :] + three_in[...]
+        one_in[direct, :] + two_in[direct, :] + three_in[parity("gx")]
     )
 
 
@@ -396,7 +409,7 @@
         out[:, q, :] = blocks_down(jnp.where(live, result[q], 0.0))
 
 
-def call(kernel, outs, scratch, specs, name, micros=1, megabytes=24.0):
+def call(kernel, outs, scratch, specs, name, micros=1):
     return pl.pallas_call(
         kernel,
         out_shape=outs if len(outs) > 1 else outs[0],
@@ -406,7 +419,7 @@
         cost_estimate=pl.CostEstimate(
             flops=int(micros * 1e9), bytes_accessed=1000000, transcendentals=0
         ),
-        compiler_params=pltpu.CompilerParams(vmem_limit_bytes=int(megabytes * 1024 * 1024)),
+        compiler_params=pltpu.CompilerParams(vmem_limit_bytes=24 * 1024 * 1024),
         name=name,
     )
 
@@ -424,12 +437,19 @@
     return [(i, (i + distance if i % 2 else i - distance) % peers) for i in range(peers)]
 
 
-def along_y(field, distance):
+def column_pairs(distance, above):
     wide, tall = lax.axis_size("gx"), lax.axis_size("gy")
+    return [
+        [(x + above) * tall + y, (x + 1 - above) * tall + (y + distance) % tall]
+        for x in range(0, wide, 2)
+        for y in range(tall)
+    ]
+
+
+def swap_y(field, distance):
     route = []
-    for x in range(wide):
-        step = -distance if x % 2 else distance
-        route += [(x * tall + y, x * tall + (y + step) % tall) for y in range(tall)]
+    for low, high in column_pairs(distance, 0):
+        route += [(low, high), (high, low)]
     return lax.ppermute(field, ("gx", "gy"), route)
 
 
@@ -453,6 +473,7 @@
     downward = downward_ops.transpose(1, 0, 2)
     index_row = pltpu.VMEM((1, LANES), jnp.int32)
 
+    atoms = (pos, charge, cell, count, upward)
     own_field = call(
         moments_kernel,
         [rows(LEAF + PAIR)],
@@ -472,20 +493,24 @@
         [HBM] * 5,
         "moments",
         3,
-        63.9,
-    )(pos, charge, cell, count, upward)
-
-    near = lax.all_gather(own_field, "gx", axis_index_groups=chip_pairs())
+    )(*[pltpu.with_memory_space_constraint(x, pltpu.HBM) for x in atoms])
+
+    both = lax.all_gather(own_field, "gx", axis_index_groups=chip_pairs())
+    near, parents = call(
+        pair_kernel, [rows(2 * LEAF + PAIR), rows(PAIR)], [], [VMEM], "pair"
+    )(both)
     beside = lax.ppermute(near, "gx", outward_x(1))
-    parents = near[0, LEAF:] + near[1, LEAF:]
     beyond = lax.ppermute(parents, "gx", outward_x(3))
     leaf_k, coarse_k = call(
         tables_kernel,
         [
             jax.ShapeDtypeStruct((12 * PAD, DEPTH), BF16),
-            jax.ShapeDtypeStruct((6 * PAD, DEPTH), BF16),
+            jax.ShapeDtypeStruct((10 * PAD, DEPTH), BF16),
         ],
-        [pltpu.VMEM((8, NZ), F32), pltpu.VMEM((TILES * PAD, 2 * NZ), F32)],
+        [
+            pltpu.VMEM((8, NZ), F32),
+            pltpu.VMEM((TILES * PAD, 2 * NZ), F32),
+        ],
         [VMEM] * 4,
         "tables",
         2,
@@ -501,16 +526,23 @@
     one, two, kept = call(
         translate_kernel,
         [rows(2 * LEAF + 2 * PAIR), rows(2 * LEAF + 2 * PAIR), rows(LEAF + 2 * PAIR)],
-        [pltpu.VMEM((6, LEAF, NZ), F32)] + [pltpu.VMEM((DEPTH, NQ * NZ), BF16)] * 2,
+        [
+            pltpu.VMEM((2, 6, LEAF, NZ), F32),
+            pltpu.VMEM((2, 5, PAIR, NZ), F32),
+            pltpu.VMEM((DEPTH, NQ * NZ), BF16),
+            pltpu.VMEM((DEPTH, NQ * NZ), BF16),
+            pltpu.VMEM((DEPTH, 2 * NZ), BF16),
+            pltpu.VMEM((DEPTH, 2 * NZ), BF16),
+        ],
         [VMEM] * 4,
         "translate",
         3,
     )(near, sides, leaf_k, coarse_k)
 
-    one = along_y(one, 1)
-    two = along_y(two, 2)
+    one = swap_y(one, 1)
+    two = swap_y(two, 2)
     relayed = call(relay_kernel, [rows(PAIR)], [], [VMEM] * 3, "relay")(kept, one, two)
-    three = along_y(relayed, 3)
+    three = lax.all_gather(relayed, ("gx", "gy"), axis_index_groups=column_pairs(3, 1))
     basis = call(
         basis_kernel,
         [jax.ShapeDtypeStruct((NP, BLKS, SLOT), F32)],

time: 58.6 us -> 56.4 us (0.962)
  starting transfers between devices: 21.3 us -> 18.2 us
  blocking collectives: 18 us -> 20.7 us
  local copies, waits for them, and re-layouts: 2.03 us -> 0.03 us
  waiting for transfers between devices: 6.22 us -> 7.65 us
  Pallas kernels: 10.5 us -> 9.32 us
    all_gather x1 -> x2, blocking collectives: 8.66 us -> 13.3 us  [the longest x1 8.45 us: per_device(): both = lax.all_gather(own_field, 'gx', axis_index_groups=chip_pairs())]
    ppermute x3 -> x2, starting transfers between devices: 17.5 us -> 13.7 us  [swap_y(): return lax.ppermute(field, ('gx', 'gy'), route)]
    all_gather x1, blocking collectives: 5.19 us -> 2.06 us  [per_device(): last = lax.all_gather(passed, 'gx', axis_index_groups=chip_pairs())]
    unnamed x16, local copies, waits for them, and re-layouts: 2.03 us -> 0.03 us
    ppermute x1, waiting for transfers between devices: 0.01 us -> 1.56 us  [per_device(): beside = lax.ppermute(near, 'gx', outward_x(1))]
    all_gather x1, blocking collectives: 4.14 us -> 5.38 us  [per_device(): sides = lax.all_gather(side, 'gx', axis_index_groups=chip_pairs())]
    pallas_call x1, Pallas kernels: 3.64 us -> 2.92 us  [per_device(): call(moments_kernel, [rows(LEAF + PAIR)], [pltpu.VMEM((BLKS, 3, SLOT), F3...]
    ppermute x1, waiting for transfers between devices: 1.59 us -> 1 us  [per_device(): beyond = lax.ppermute(parents, 'gx', outward_x(3))]
  transfers between devices with their start and end apart: 5 -> 4, of which waited for: 3 -> 4; matrix products, arithmetic and copies ran while one was open for 0% -> 0% of each run, Pallas kernels for 3% -> 4%
where the time goes in v1:
time: 56.4 us; the launch traced here: 56.1 us
  blocking collectives  20.7 us (37%)
  starting transfers between devices  18.2 us (32%)
  Pallas kernels  9.32 us (17%)
  waiting for transfers between devices  7.65 us (14%)
    ppermute x2, starting transfers between devices, swap_y(): return lax.ppermute(field, ('gx', 'gy'), route)  13.7 us
    all_gather x1, blocking collectives, per_device(): both = lax.all_gather(own_field, 'gx', axis_index_groups=chip_pairs())  8.45 us
    all_gather x1, blocking collectives, per_device(): sides = lax.all_gather(side, 'gx', axis_index_groups=chip_pairs())  5.38 us
    ppermute x2, waiting for transfers between devices, swap_y(): return lax.ppermute(field, ('gx', 'gy'), route)  5.09 us
    all_gather x1, blocking collectives, per_device(): lax.all_gather(relayed, ('gx', 'gy'), axis_index_groups=column_pairs(3, 1))  4.87 us
    pallas_call x1, Pallas kernels, per_device(): call(moments_kernel, [rows(LEAF + PAIR)], [pltpu.VMEM((BLKS, 3, SLOT), F3...  2.92 us
    ppermute x1, starting transfers between devices, per_device(): beside = lax.ppermute(near, 'gx', outward_x(1))  2.48 us
    pallas_call x1, Pallas kernels, per_device(): call(potential_kernel, [jax.ShapeDtypeStruct((BLKS, NQ, SLOT), F32)], [in...  2.2 us
  transfers between devices with their start and end apart: 4, of which 4 were waited for; matrix products, arithmetic and copies ran while one was open for 0% of the time, Pallas kernels for 4%

profile of v1, /device:TPU:1, one launch (start us, length us, event | category | flops | bytes accessed | tf_op | source)
XLA Modules:
  0.0 56.1 jit_solution(2585888074453218526)
XLA Ops:
  0.0 2.9 %moments.1 = f32[160,128]{1,0:T(8,128)S(1)} custom-call(f32[160,3,128]{2,1,0:T(4,128)} %bitcast.27, f32[160,4,128]{2,1,0:T(4,128)} %bitcast.36, s32[1,160]{1,0:T(1,128)} %bitcast.32, s32[1,160]{1,0:T(1,128)} %bitcast.34, f32[25,8,25]{2,1,0:T(8,128)} %bitcast.37), custom_call_target="tpu_custom_call" | custom-call | flops 3000000000 | bytes 1000000 | tf_op jit(solution)/shard_map/moments/pallas_call | solution.py:477
  2.9 8.4 %all-gather = f32[320,128]{1,0:T(8,128)S(1)} all-gather(f32[160,128]{1,0:T(8,128)S(1)} %moments.1), channel_id=2, replica_groups={{0,32},{64,96},{128,160},{192,224},{256,288},{320,352},{384,416},{448,4..., dimensions={0}, use_global_device_ids=true | all-gather | bytes 245760 | tf_op jit(solution)/shard_map/all_gather | solution.py:498
  11.4 0.0 copy-start
  11.4 0.0 copy-start.1
  11.4 0.0 copy-start.4
  11.4 0.0 copy-start.5
  11.4 2.1 %collective-permute-start.1 = (f32[56,128]{1,0:T(8,128)S(1)}, f32[56,128]{1,0:T(8,128)S(1)}, u32[]{:S(2)}, u32[]{:S(2)}) collective-permute-start(f32[56,128]{1,0:T(8,128)S(1)} %get-tuple-element.13), channel_id=1, source_target_pairs={{0,416},{32,128},{64,480},{96,192},{128,32},{160,256},{192,96},{22... | collective-permute-start | bytes 86024 | tf_op jit(solution)/shard_map/ppermute | solution.py:503
  13.5 2.5 %collective-permute-start = (f32[264,128]{1,0:T(8,128)S(1)}, f32[264,128]{1,0:T(8,128)S(1)}, u32[]{:S(2)}, u32[]{:S(2)}) collective-permute-start(f32[264,128]{1,0:T(8,128)S(1)} %get-tuple-element.12.near), channel_id=1, source_target_pairs={{0,480},{32,64},{64,32},{96,128},{128,96},{160,192},{192,160},{224... | collective-permute-start | bytes 405512 | tf_op jit(solution)/shard_map/ppermute | solution.py:502
  16.0 0.0 copy-done
  16.0 0.0 copy-done.1
  16.0 0.0 copy-done.4
  16.0 0.0 copy-done.5
  16.0 1.5 %tables.1 = (bf16[384,1664]{1,0:T(8,128)(2,1)S(1)}, bf16[320,1664]{1,0:T(8,128)(2,1)S(1)}) custom-call(s32[3,96]{1,0:T(4,128)S(1)} %bitcast.30, s32[3,96]{1,0:T(4,128)S(1)} %bitcast.31, f32[25,25,96]{2,1,0:T(8,128)S(1)} %bitcast.25, f32[25,25,96]{2,1,0:T(8,128)S(1)} %bitcast.26), custom_call_target="tpu_custom_call" | custom-call | flops 2000000000 | bytes 1000000 | tf_op jit(solution)/shard_map/tables/pallas_call | solution.py:504
  17.5 1.0 %collective-permute-done.1.far = f32[56,128]{1,0:T(8,128)S(1)} collective-permute-done((f32[56,128]{1,0:T(8,128)S(1)}, f32[56,128]{1,0:T(8,128)S(1)}, u32[]{:S(2)}, u32[]{:S(2)}) %collective-permute-start.1) | collective-permute-done | bytes 28704 | tf_op jit(solution)/shard_map/ppermute | solution.py:503
  18.5 1.6 %collective-permute-done.fields = f32[264,128]{1,0:T(8,128)S(1)} collective-permute-done((f32[264,128]{1,0:T(8,128)S(1)}, f32[264,128]{1,0:T(8,128)S(1)}, u32[]{:S(2)}, u32[]{:S(2)}) %collective-permute-start) | collective-permute-done | bytes 135200 | tf_op jit(solution)/shard_map/ppermute | solution.py:502
  20.1 5.4 %all-gather.1 = f32[640,128]{1,0:T(8,128)S(1)} all-gather(f32[320,128]{1,0:T(8,128)S(1)} %join.1), channel_id=3, replica_groups={{0,32},{64,96},{128,160},{192,224},{256,288},{320,352},{384,416},{448,4..., dimensions={0}, use_global_device_ids=true | all-gather | bytes 491520 | tf_op jit(solution)/shard_map/all_gather | solution.py:524
  25.5 0.0 copy-start.2
  25.5 2.1 %translate.1 = (f32[320,128]{1,0:T(8,128)S(1)}, f32[320,128]{1,0:T(8,128)S(1)}, f32[216,128]{1,0:T(8,128)S(1)}) custom-call(f32[264,128]{1,0:T(8,128)S(1)} %get-tuple-element.12.near, f32[2,320,128]{2,1,0:T(8,128)S(1)} %bitcast.21, bf16[384,1664]{1,0:T(8,128)(2,1)S(1)} %get-tuple-element.14.leaf_k, bf16[320,1664]{1,0:T(8,128)(2,1)S(1)} %get-tuple-element.15.coarse_k), custom_call_target="tpu_custom_call" | custom-call | flops 3000000000 | bytes 1000000 | tf_op jit(solution)/shard_map/translate/pallas_call | solution.py:526
  27.6 11.5 %collective-permute-start.2 = (f32[320,128]{1,0:T(8,128)S(1)}, f32[320,128]{1,0:T(8,128)S(1)}, u32[]{:S(2)}, u32[]{:S(2)}) collective-permute-start(f32[320,128]{1,0:T(8,128)S(1)} %get-tuple-element.17), channel_id=1, source_target_pairs={{0,33},{33,0},{1,34},{34,1},{2,35},{35,2},{3,36},{36,3},{4,37},{37... | collective-permute-start | bytes 491528 | tf_op jit(solution)/shard_map/ppermute | solution.py:453
  39.1 2.2 %collective-permute-start.3 = (f32[320,128]{1,0:T(8,128)S(1)}, f32[320,128]{1,0:T(8,128)S(1)}, u32[]{:S(2)}, u32[]{:S(2)}) collective-permute-start(f32[320,128]{1,0:T(8,128)S(1)} %get-tuple-element.18), channel_id=1, source_target_pairs={{0,34},{34,0},{1,35},{35,1},{2,36},{36,2},{3,37},{37,3},{4,38},{38... | collective-permute-start | bytes 491528 | tf_op jit(solution)/shard_map/ppermute | solution.py:453
  41.3 0.0 copy-done.2
  41.3 0.5 basis.1
  41.8 0.2 collective-permute-done.2.one_in
  42.1 4.9 %collective-permute-done.3.two_in = f32[320,128]{1,0:T(8,128)S(1)} collective-permute-done((f32[320,128]{1,0:T(8,128)S(1)}, f32[320,128]{1,0:T(8,128)S(1)}, u32[]{:S(2)}, u32[]{:S(2)}) %collective-permute-start.3) | collective-permute-done | bytes 163872 | tf_op jit(solution)/shard_map/ppermute | solution.py:453
  46.9 4.9 %all-gather.2 = f32[112,128]{1,0:T(8,128)S(1)} all-gather(f32[56,128]{1,0:T(8,128)S(1)} %relay.1), channel_id=4, replica_groups={{32,3},{33,4},{34,5},{35,6},{36,7},{37,8},{38,9},{39,10},{40,11},{41,12..., dimensions={0}, use_global_device_ids=true | all-gather | bytes 86016 | tf_op jit(solution)/shard_map/all_gather | solution.py:545
  51.8 0.0 copy-start.3
  51.8 0.0 copy-start.6
  51.8 0.0 copy-start.7
  51.8 2.1 %all-gather.3 = f32[320,128]{1,0:T(8,128)S(1)} all-gather(f32[160,128]{1,0:T(8,128)S(1)} %exchange.1), channel_id=5, replica_groups={{0,32},{64,96},{128,160},{192,224},{256,288},{320,352},{384,416},{448,4..., dimensions={0}, use_global_device_ids=true | all-gather | bytes 245760 | tf_op jit(solution)/shard_map/all_gather | solution.py:556
  53.9 0.0 copy-done.3
  53.9 0.0 copy-done.6
  53.9 0.0 copy-done.7
  53.9 2.2 %potential.1 = f32[160,4,128]{2,1,0:T(4,128)} custom-call(f32[216,128]{1,0:T(8,128)S(1)} %get-tuple-element.16.kept.after, f32[320,128]{1,0:T(8,128)S(1)} %collective-permute-done.2.one_in, f32[320,128]{1,0:T(8,128)S(1)} %collective-permute-done.3.two_in, f32[2,160,128]{2,1,0:T(8,128)S(1)} %bitcast.22, s32[1,160]{1,0:T(1,128)S(1)} %bitcast.33, ...), custom_call_target="tpu_custom_call" | custom-call | flops 3000000000 | bytes 1000000 | tf_op jit(solution)/shard_map/potential/pallas_call | solution.py:558
  (4 shorter events, 0.1 us)
Async XLA Ops:
  11.4 4.6 %copy-start = (f32[96,25,25]{0,2,1:T(8,128)S(1)}, f32[96,25,25]{0,2,1:T(8,128)}, u32[]{:S(2)}) copy-start(f32[96,25,25]{0,2,1:T(8,128)} %param.16) | copy-start | bytes 720004
  11.4 4.6 %copy-start.1 = (f32[96,25,25]{0,2,1:T(8,128)S(1)}, f32[96,25,25]{0,2,1:T(8,128)}, u32[]{:S(2)}) copy-start(f32[96,25,25]{0,2,1:T(8,128)} %param.17) | copy-start | bytes 720004
  11.4 4.6 %copy-start.4 = (s32[96,3]{0,1:T(4,128)S(1)}, s32[96,3]{0,1:T(4,128)}, u32[]{:S(2)}) copy-start(s32[96,3]{0,1:T(4,128)} %param.14) | copy-start | bytes 3460
  11.4 4.6 %copy-start.5 = (s32[96,3]{0,1:T(4,128)S(1)}, s32[96,3]{0,1:T(4,128)}, u32[]{:S(2)}) copy-start(s32[96,3]{0,1:T(4,128)} %param.15) | copy-start | bytes 3460
  11.4 7.1 %collective-permute-start.1 = (f32[56,128]{1,0:T(8,128)S(1)}, f32[56,128]{1,0:T(8,128)S(1)}, u32[]{:S(2)}, u32[]{:S(2)}) collective-permute-start(f32[56,128]{1,0:T(8,128)S(1)} %get-tuple-element.13), channel_id=1, source_target_pairs={{0,416},{32,128},{64,480},{96,192},{128,32},{160,256},{192,96},{22... | collective-permute-start | bytes 86024 | tf_op jit(solution)/shard_map/ppermute | solution.py:503
  13.5 6.6 %collective-permute-start = (f32[264,128]{1,0:T(8,128)S(1)}, f32[264,128]{1,0:T(8,128)S(1)}, u32[]{:S(2)}, u32[]{:S(2)}) collective-permute-start(f32[264,128]{1,0:T(8,128)S(1)} %get-tuple-element.12.near), channel_id=1, source_target_pairs={{0,480},{32,64},{64,32},{96,128},{128,96},{160,192},{192,160},{224... | collective-permute-start | bytes 405512 | tf_op jit(solution)/shard_map/ppermute | solution.py:502
  25.5 15.8 %copy-start.2 = (f32[3,20480]{1,0:T(4,128)S(1)}, f32[3,20480]{1,0:T(4,128)}, u32[]{:S(2)}) copy-start(f32[3,20480]{1,0:T(4,128)} %param.10) | copy-start | bytes 737284
  27.6 14.5 %collective-permute-start.2 = (f32[320,128]{1,0:T(8,128)S(1)}, f32[320,128]{1,0:T(8,128)S(1)}, u32[]{:S(2)}, u32[]{:S(2)}) collective-permute-start(f32[320,128]{1,0:T(8,128)S(1)} %get-tuple-element.17), channel_id=1, source_target_pairs={{0,33},{33,0},{1,34},{34,1},{2,35},{35,2},{3,36},{36,3},{4,37},{37... | collective-permute-start | bytes 491528 | tf_op jit(solution)/shard_map/ppermute | solution.py:453
  39.1 7.8 %collective-permute-start.3 = (f32[320,128]{1,0:T(8,128)S(1)}, f32[320,128]{1,0:T(8,128)S(1)}, u32[]{:S(2)}, u32[]{:S(2)}) collective-permute-start(f32[320,128]{1,0:T(8,128)S(1)} %get-tuple-element.18), channel_id=1, source_target_pairs={{0,34},{34,0},{1,35},{35,1},{2,36},{36,2},{3,37},{37,3},{4,38},{38... | collective-permute-start | bytes 491528 | tf_op jit(solution)/shard_map/ppermute | solution.py:453
  51.8 2.1 %copy-start.3 = (f32[8,25,25]{2,0,1:T(8,128)S(1)}, f32[8,25,25]{2,0,1:T(8,128)}, u32[]{:S(2)}) copy-start(f32[8,25,25]{2,0,1:T(8,128)} %param.19) | copy-start | bytes 60004
  51.8 2.1 %copy-start.6 = (s32[160]{0:T(256)S(1)}, s32[160]{0:T(256)}, u32[]{:S(2)}) copy-start(s32[160]{0:T(256)} %param.12) | copy-start | bytes 1924
  51.8 2.1 %copy-start.7 = (s32[160]{0:T(256)S(1)}, s32[160]{0:T(256)}, u32[]{:S(2)}) copy-start(s32[160]{0:T(256)} %param.13) | copy-start | bytes 1924

commit v2 on v1

--- a/solution.py
+++ b/solution.py
@@ -18,8 +18,8 @@
 PAD = 32
 LEAF = 104
 PAIR = 56
-GROUP = 48
-TILES = 13
+GROUP = 32
+TILES = 7
 DEPTH = TILES * NZ
 F32 = jnp.float32
 BF16 = jnp.bfloat16
@@ -214,47 +214,54 @@
         store_packed(out, LEAF, pair, 2, value)
 
 
-def tables_kernel(leaf_at, coarse_at, leaf_ops, coarse_ops, leaf_out, coarse_out, codes, left):
+def tables_kernel(leaf_at, coarse_at, leaf_ops, coarse_ops, *refs):
+    codes, left = refs[4:]
     toward = (1 - 2 * parity("gx")).astype(F32)
     lane = lax.broadcasted_iota(jnp.int32, (NZ, NZ), 1).astype(F32)
-    for at, ops, out, columns in (
-        (leaf_at, leaf_ops, leaf_out, 2),
-        (coarse_at, coarse_ops, coarse_out, 1),
+    for at, ops, outs, columns, reaches in (
+        (leaf_at, leaf_ops, refs[0:2], 2, (0, 1, 2)),
+        (coarse_at, coarse_ops, refs[2:4], 1, (0, 1, 2, -1, -2)),
     ):
-        reaches = (0, 1, 2) if columns == 2 else (0, 1, 2, -1, -2)
         codes[...] = jnp.full((8, NZ), 99.0, F32)
         codes[0:3, 0:CLS] = at[...].astype(F32)
         turned = codes[...].T
-        place = (turned[:, 0:1] + 2.0) * 8.0 + 3.0 - turned[:, 2:3]
-        ahead = -toward * turned[:, 1:2]
+        ahead = [-toward * turned[:, 1:2] == float(r) for r in reaches]
+        places = []
+        for own in (True, False):
+            for t in range(columns):
+                source = turned[:, 0:1] + float(2 + t)
+                near = (source >= 2.0) & (source < float(2 + columns))
+                if own:
+                    chosen, column = near, source - 2.0
+                else:
+                    chosen = jnp.logical_not(near)
+                    column = jnp.where(source < 2.0, source, source - float(columns))
+                place = column * 8.0 + 3.0 - turned[:, 2:3]
+                places.append(jnp.where(chosen, place, -1000.0))
         picks = []
-        for half in range(2):
-            found = [lane == place + float(half * GROUP + t * 8) for t in range(columns)]
-            picks.append(
-                jnp.concatenate(
-                    [
-                        (found[t] & (ahead == float(r))).astype(F32)
-                        for t in range(columns)
-                        for r in reaches
-                    ],
-                    axis=1,
-                )
-            )
-        pick = jnp.concatenate(picks, axis=0).astype(BF16)
+        for part in range(4):
+            blocks = []
+            for place in places:
+                found = lane == place + float(part * GROUP)
+                blocks += [(found & row).astype(BF16) for row in ahead]
+            picks.append(jnp.concatenate(blocks, axis=1))
+        pick = jnp.concatenate(picks, axis=0)
         left[...] = jnp.zeros_like(left)
         for i in range(NP):
-            row = (i // 2) * PAD
-            col = (i % 2) * NZ
+            row = (i // 4) * PAD
+            col = (i % 4) * NZ
             left[row : row + NP, col : col + CLS] = ops[:, i, :]
         blocks = columns * len(reaches)
         for part, value in enumerate(split(left[...])):
             table = dot(value, pick).astype(BF16)
-            for tile in range(TILES):
-                for block in range(blocks):
-                    row = (part * blocks + block) * PAD
-                    out[row : row + PAD, tile * NZ : (tile + 1) * NZ] = table[
-                        tile * PAD : (tile + 1) * PAD, block * NZ : (block + 1) * NZ
-                    ]
+            for side, out in enumerate(outs):
+                for tile in range(TILES):
+                    for block in range(blocks):
+                        row = (part * blocks + block) * PAD
+                        col = (side * blocks + block) * NZ
+                        out[row : row + PAD, tile * NZ : (tile + 1) * NZ] = table[
+                            tile * PAD : (tile + 1) * PAD, col : col + NZ
+                        ]
 
 
 def pair_kernel(near, fields, parents):
@@ -270,68 +277,80 @@
     out[2 * LEAF + PAIR :, :] = far[...]
 
 
-def translate_kernel(near, sides, leaf_k, coarse_k, one_out, two_out, kept, *scratch):
+def back(target, column, value, step):
+    value = pltpu.roll(value, NZ - 3 * step, 1)
+    top = value.astype(BF16).astype(F32)
+    target[0, column] = top
+    target[1, column] = value - top
+
+
+def spread(source, columns, high, low, step):
+    channels = high.shape[1] // NZ
+    used = NP * GROUP
+    for ref in (high, low):
+        ref[used:, :] = jnp.zeros((DEPTH - used, ref.shape[1]), BF16)
+
+    def turned(part, column, at):
+        if column is None:
+            return jnp.zeros((8, NZ), F32)
+        value = jnp.broadcast_to(source[part, column, at : at + 1, :], (8, NZ))
+        return pltpu.roll(value, 0, 1, stride=step, stride_axis=0)
+
+    for i in range(NP):
+        for two in range(2):
+            base = i * GROUP + two * 16
+            members = columns[2 * two : 2 * two + 2]
+            for part, ref in enumerate((high, low)):
+                if not members:
+                    ref[base : base + 16, :] = jnp.zeros((16, ref.shape[1]), BF16)
+                    continue
+                for q in range(channels):
+                    at = q * 24 + i if i < 24 else channels * 24 + q
+                    value = jnp.concatenate(
+                        [turned(part, column, at) for column in members], axis=0
+                    )
+                    ref[base : base + 16, q * NZ : (q + 1) * NZ] = value.astype(BF16)
+
+
+def product(table, high, low):
+    height = table.shape[0] // 2
+    both = dot(table[...], high[...])
+    return both[:height] + both[height:] + dot(table[0:height, :], low[...])
+
+
+def own_kernel(near, leaf_k, coarse_k, leaf_out, coarse_out, *scratch):
     fields, parents, high, low, coarse_high, coarse_low = scratch
+    back(parents, 0, near[2 * LEAF :, :], 2)
+    for a in range(2):
+        back(fields, a, near[a * LEAF : (a + 1) * LEAF, :], 1)
+    spread(parents, [0, None], coarse_high, coarse_low, 2)
+    spread(fields, [0, 1], high, low, 1)
+    coarse_out[...] = product(coarse_k, coarse_high, coarse_low)
+    leaf_out[...] = product(leaf_k, high, low)
+
+
+def translate_kernel(sides, leaf_k, coarse_k, own_leaf, own_coarse, *refs):
+    one_out, two_out, kept, fields, parents, high, low, coarse_high, coarse_low = refs
     core = parity("gx")
-    for ref in (high, low, coarse_high, coarse_low):
-        for tile in range(TILES):
-            used = 2 * GROUP if 2 * tile + 1 < NP else GROUP
-            ref[tile * NZ + used : (tile + 1) * NZ, :] = jnp.zeros(
-                (NZ - used, ref.shape[1]), BF16
-            )
-
-    def spread(source, columns, high, low, step):
-        channels = high.shape[1] // NZ
-
-        def turned(part, column, at):
-            if column is None:
-                return jnp.zeros((8, NZ), F32)
-            value = jnp.broadcast_to(source[part, column, at : at + 1, :], (8, NZ))
-            return pltpu.roll(value, 0, 1, stride=step, stride_axis=0)
-
-        for i in range(NP):
-            row = (i // 2) * NZ + (i % 2) * GROUP
-            for q in range(channels):
-                at = q * 24 + i if i < 24 else channels * 24 + q
-                for two in range(3):
-                    base = row + two * 16
-                    for part, ref in enumerate((high, low)):
-                        value = jnp.concatenate(
-                            [turned(part, column, at) for column in columns[2 * two : 2 * two + 2]],
-                            axis=0,
-                        )
-                        ref[base : base + 16, q * NZ : (q + 1) * NZ] = value.astype(BF16)
-
-    def product(table, height, high, low):
-        both = dot(table[...], high[...])
-        return both[:height] + both[height:] + dot(table[0:height, :], low[...])
 
     def emit(ref, base, value, channels, rows):
         ref[base + channels * 25 : base + rows, :] = jnp.zeros((rows - channels * 25, NZ), F32)
         for q in range(channels):
             store_packed(ref, base, q, channels, value[:, q * NZ : (q + 1) * NZ])
 
-    def back(target, column, value, step):
-        value = pltpu.roll(value, NZ - 3 * step, 1)
-        top = value.astype(BF16).astype(F32)
-        target[0, column] = top
-        target[1, column] = value - top
-
     one, two = 2 * LEAF, 2 * LEAF + PAIR
     back(parents, 0, sides[0, two:, :], 2)
     back(parents, 1, sides[0, one:two, :], 2)
-    back(parents, 2, near[one:, :], 2)
-    back(parents, 3, sides[1, one:two, :], 2)
-    back(parents, 4, sides[1, two:, :], 2)
+    back(parents, 2, sides[1, one:two, :], 2)
+    back(parents, 3, sides[1, two:, :], 2)
     for a in range(2):
         back(fields, a, sides[0, a * LEAF : (a + 1) * LEAF, :], 1)
-        back(fields, 2 + a, near[a * LEAF : (a + 1) * LEAF, :], 1)
-        back(fields, 4 + a, sides[1, a * LEAF : (a + 1) * LEAF, :], 1)
-    spread(parents, [0, 1, 2, 3, 4, None], coarse_high, coarse_low, 2)
-    spread(fields, range(6), high, low, 1)
-    result = product(coarse_k, 5 * PAD, coarse_high, coarse_low)
+        back(fields, 2 + a, sides[1, a * LEAF : (a + 1) * LEAF, :], 1)
+    spread(parents, [0, 1, 2, 3], coarse_high, coarse_low, 2)
+    spread(fields, [0, 1, 2, 3], high, low, 1)
+    result = product(coarse_k, coarse_high, coarse_low) + own_coarse[...]
     coarse = [result[b * PAD : (b + 1) * PAD] for b in range(5)]
-    result = product(leaf_k, 6 * PAD, high, low)
+    result = product(leaf_k, high, low) + own_leaf[...]
     blocks = [result[b * PAD : (b + 1) * PAD] for b in range(6)]
     for t in range(2):
         emit(one_out, t * LEAF, blocks[3 * t + 1], NQ, LEAF)
@@ -453,6 +472,17 @@
     return lax.ppermute(field, ("gx", "gy"), route)
 
 
+def translation_scratch(leaf_columns, coarse_columns):
+    return [
+        pltpu.VMEM((2, leaf_columns, LEAF, NZ), F32),
+        pltpu.VMEM((2, coarse_columns, PAIR, NZ), F32),
+        pltpu.VMEM((DEPTH, NQ * NZ), BF16),
+        pltpu.VMEM((DEPTH, NQ * NZ), BF16),
+        pltpu.VMEM((DEPTH, 2 * NZ), BF16),
+        pltpu.VMEM((DEPTH, 2 * NZ), BF16),
+    ]
+
+
 def per_device(
     rel_pos,
     charges,
@@ -501,16 +531,12 @@
     )(both)
     beside = lax.ppermute(near, "gx", outward_x(1))
     beyond = lax.ppermute(parents, "gx", outward_x(3))
-    leaf_k, coarse_k = call(
+    leaf_table = jax.ShapeDtypeStruct((12 * PAD, DEPTH), BF16)
+    coarse_table = jax.ShapeDtypeStruct((10 * PAD, DEPTH), BF16)
+    leaf_near, leaf_far, coarse_near, coarse_far = call(
         tables_kernel,
-        [
-            jax.ShapeDtypeStruct((12 * PAD, DEPTH), BF16),
-            jax.ShapeDtypeStruct((10 * PAD, DEPTH), BF16),
-        ],
-        [
-            pltpu.VMEM((8, NZ), F32),
-            pltpu.VMEM((TILES * PAD, 2 * NZ), F32),
-        ],
+        [leaf_table, leaf_table, coarse_table, coarse_table],
+        [pltpu.VMEM((8, NZ), F32), pltpu.VMEM((TILES * PAD, 4 * NZ), F32)],
         [VMEM] * 4,
         "tables",
         2,
@@ -520,24 +546,28 @@
         leaf_ops.transpose(1, 2, 0),
         coarse_ops.transpose(1, 2, 0),
     )
+    own_leaf, own_coarse = call(
+        own_kernel,
+        [
+            jax.ShapeDtypeStruct((6 * PAD, NQ * NZ), F32),
+            jax.ShapeDtypeStruct((5 * PAD, 2 * NZ), F32),
+        ],
+        translation_scratch(2, 1),
+        [VMEM] * 3,
+        "own",
+        2,
+    )(near, leaf_near, coarse_near)
     side = call(join_kernel, [rows(2 * LEAF + 2 * PAIR)], [], [VMEM] * 2, "join")(beside, beyond)
     sides = lax.all_gather(side, "gx", axis_index_groups=chip_pairs())
 
     one, two, kept = call(
         translate_kernel,
         [rows(2 * LEAF + 2 * PAIR), rows(2 * LEAF + 2 * PAIR), rows(LEAF + 2 * PAIR)],
-        [
-            pltpu.VMEM((2, 6, LEAF, NZ), F32),
-            pltpu.VMEM((2, 5, PAIR, NZ), F32),
-            pltpu.VMEM((DEPTH, NQ * NZ), BF16),
-            pltpu.VMEM((DEPTH, NQ * NZ), BF16),
-            pltpu.VMEM((DEPTH, 2 * NZ), BF16),
-            pltpu.VMEM((DEPTH, 2 * NZ), BF16),
-        ],
-        [VMEM] * 4,
+        translation_scratch(4, 4),
+        [VMEM] * 5,
         "translate",
         3,
-    )(near, sides, leaf_k, coarse_k)
+    )(sides, leaf_far, coarse_far, own_leaf, own_coarse)
 
     one = swap_y(one, 1)
     two = swap_y(two, 2)

time: 56.4 us -> 54.9 us (0.973)
  Pallas kernels: 9.32 us -> 11 us
  waiting for transfers between devices: 7.65 us -> 6.49 us
  blocking collectives: 20.7 us -> 19.6 us
  starting transfers between devices: 18.2 us -> 17.3 us
    pallas_call x1 -> x2, Pallas kernels: 1.53 us -> 3.61 us  [the longest x1 2.33 us: per_device(): call(tables_kernel, [leaf_table, leaf_table, coarse_table, coarse_table],...]
    ppermute x1, waiting for transfers between devices: 1.56 us -> 0.01 us  [per_device(): beside = lax.ppermute(near, 'gx', outward_x(1))]
    all_gather x1, blocking collectives: 5.38 us -> 4.14 us  [per_device(): sides = lax.all_gather(side, 'gx', axis_index_groups=chip_pairs())]
    pallas_call x1, Pallas kernels: 2.1 us -> 1.48 us  [per_device(): call(translate_kernel, [rows(2 * LEAF + 2 * PAIR), rows(2 * LEAF + 2 * PA...]
  transfers between devices with their start and end apart: 4 -> 4, of which waited for: 4 -> 3; matrix products, arithmetic and copies ran while one was open for 0% -> 0% of each run, Pallas kernels for 4% -> 8%
where the time goes in v2:
time: 54.9 us; the launch traced here: 54.6 us
  blocking collectives  19.6 us (36%)
  starting transfers between devices  17.3 us (32%)
  Pallas kernels  11 us (20%)
  waiting for transfers between devices  6.49 us (12%)
    ppermute x2, starting transfers between devices, swap_y(): return lax.ppermute(field, ('gx', 'gy'), route)  13.5 us
    all_gather x1, blocking collectives, per_device(): both = lax.all_gather(own_field, 'gx', axis_index_groups=chip_pairs())  8.58 us
    ppermute x2, waiting for transfers between devices, swap_y(): return lax.ppermute(field, ('gx', 'gy'), route)  5.09 us
    all_gather x1, blocking collectives, per_device(): lax.all_gather(relayed, ('gx', 'gy'), axis_index_groups=column_pairs(3, 1))  5 us
    all_gather x1, blocking collectives, per_device(): sides = lax.all_gather(side, 'gx', axis_index_groups=chip_pairs())  4.14 us
    pallas_call x1, Pallas kernels, per_device(): call(moments_kernel, [rows(LEAF + PAIR)], [pltpu.VMEM((BLKS, 3, SLOT), F3...  2.92 us
    pallas_call x1, Pallas kernels, per_device(): call(potential_kernel, [jax.ShapeDtypeStruct((BLKS, NQ, SLOT), F32)], [in...  2.41 us
    pallas_call x1, Pallas kernels, per_device(): call(tables_kernel, [leaf_table, leaf_table, coarse_table, coarse_table],...  2.33 us
  transfers between devices with their start and end apart: 4, of which 3 were waited for; matrix products, arithmetic and copies ran while one was open for 0% of the time, Pallas kernels for 8%

profile of v2, /device:TPU:1, one launch (start us, length us, event | category | flops | bytes accessed | tf_op | source)
XLA Modules:
  0.0 54.6 jit_solution(13284642374827161326)
XLA Ops:
  0.0 2.9 %moments.1 = f32[160,128]{1,0:T(8,128)S(1)} custom-call(f32[160,3,128]{2,1,0:T(4,128)} %bitcast.27, f32[160,4,128]{2,1,0:T(4,128)} %bitcast.36, s32[1,160]{1,0:T(1,128)} %bitcast.32, s32[1,160]{1,0:T(1,128)} %bitcast.34, f32[25,8,25]{2,1,0:T(8,128)} %bitcast.37), custom_call_target="tpu_custom_call" | custom-call | flops 3000000000 | bytes 1000000 | tf_op jit(solution)/shard_map/moments/pallas_call | solution.py:507
  2.9 0.0 copy-start
  2.9 0.0 copy-start.1
  3.0 0.0 copy-start.4
  3.0 0.0 copy-start.5
  3.0 8.6 %all-gather = f32[320,128]{1,0:T(8,128)S(1)} all-gather(f32[160,128]{1,0:T(8,128)S(1)} %moments.1), channel_id=2, replica_groups={{0,32},{64,96},{128,160},{192,224},{256,288},{320,352},{384,416},{448,4..., dimensions={0}, use_global_device_ids=true | all-gather | bytes 245760 | tf_op jit(solution)/shard_map/all_gather | solution.py:528
  11.6 1.9 %collective-permute-start = (f32[264,128]{1,0:T(8,128)S(1)}, f32[264,128]{1,0:T(8,128)S(1)}, u32[]{:S(2)}, u32[]{:S(2)}) collective-permute-start(f32[264,128]{1,0:T(8,128)S(1)} %get-tuple-element.16.near), channel_id=1, source_target_pairs={{0,480},{32,64},{64,32},{96,128},{128,96},{160,192},{192,160},{224... | collective-permute-start | bytes 405512 | tf_op jit(solution)/shard_map/ppermute | solution.py:532
  13.5 1.9 %collective-permute-start.1 = (f32[56,128]{1,0:T(8,128)S(1)}, f32[56,128]{1,0:T(8,128)S(1)}, u32[]{:S(2)}, u32[]{:S(2)}) collective-permute-start(f32[56,128]{1,0:T(8,128)S(1)} %get-tuple-element.17), channel_id=1, source_target_pairs={{0,416},{32,128},{64,480},{96,192},{128,32},{160,256},{192,96},{22... | collective-permute-start | bytes 86024 | tf_op jit(solution)/shard_map/ppermute | solution.py:533
  15.4 0.0 copy-done
  15.4 0.0 copy-done.1
  15.5 0.0 copy-done.4
  15.5 0.0 copy-done.5
  15.5 2.3 %tables.1 = (bf16[384,896]{1,0:T(8,128)(2,1)S(1)}, bf16[384,896]{1,0:T(8,128)(2,1)S(1)}, bf16[320,896]{1,0:T(8,128)(2,1)S(1)}, bf16[320,896]{1,0:T(8,128)(2,1)S(1)}) custom-call(s32[3,96]{1,0:T(4,128)S(1)} %bitcast.30, s32[3,96]{1,0:T(4,128)S(1)} %bitcast.31, f32[25,25,96]{2,1,0:T(8,128)S(1)} %bitcast.25, f32[25,25,96]{2,1,0:T(8,128)S(1)} %bitcast.26), custom_call_target="tpu_custom_call" | custom-call | flops 2000000000 | bytes 1000000 | tf_op jit(solution)/shard_map/tables/pallas_call | solution.py:536
  17.8 1.3 %own.1 = (f32[192,512]{1,0:T(8,128)S(1)}, f32[160,256]{1,0:T(8,128)S(1)}) custom-call(f32[264,128]{1,0:T(8,128)S(1)} %get-tuple-element.16.near, bf16[384,896]{1,0:T(8,128)(2,1)S(1)} %get-tuple-element.20.leaf_k, bf16[320,896]{1,0:T(8,128)(2,1)S(1)} %get-tuple-element.21.coarse_k), custom_call_target="tpu_custom_call" | custom-call | flops 2000000000 | bytes 1000000 | tf_op jit(solution)/shard_map/own/pallas_call | solution.py:549
  19.1 1.4 %collective-permute-done.1.far = f32[56,128]{1,0:T(8,128)S(1)} collective-permute-done((f32[56,128]{1,0:T(8,128)S(1)}, f32[56,128]{1,0:T(8,128)S(1)}, u32[]{:S(2)}, u32[]{:S(2)}) %collective-permute-start.1) | collective-permute-done | bytes 28704 | tf_op jit(solution)/shard_map/ppermute | solution.py:533
  20.5 0.0 collective-permute-done.fields
  20.5 4.1 %all-gather.1 = f32[640,128]{1,0:T(8,128)S(1)} all-gather(f32[320,128]{1,0:T(8,128)S(1)} %join.1), channel_id=3, replica_groups={{0,32},{64,96},{128,160},{192,224},{256,288},{320,352},{384,416},{448,4..., dimensions={0}, use_global_device_ids=true | all-gather | bytes 491520 | tf_op jit(solution)/shard_map/all_gather | solution.py:561
  24.7 0.0 copy-start.2
  24.7 1.5 %translate.1 = (f32[320,128]{1,0:T(8,128)S(1)}, f32[320,128]{1,0:T(8,128)S(1)}, f32[216,128]{1,0:T(8,128)S(1)}) custom-call(f32[2,320,128]{2,1,0:T(8,128)S(1)} %bitcast.21, bf16[384,896]{1,0:T(8,128)(2,1)S(1)} %get-tuple-element.18.leaf_k, bf16[320,896]{1,0:T(8,128)(2,1)S(1)} %get-tuple-element.19.coarse_k, f32[192,512]{1,0:T(8,128)S(1)} %get-tuple-element.22.own_leaf, ...), custom_call_target="tpu_custom_call" | custom-call | flops 3000000000 | bytes 1000000 | tf_op jit(solution)/shard_map/translate/pallas_call | solution.py:563
  26.1 11.2 %collective-permute-start.2 = (f32[320,128]{1,0:T(8,128)S(1)}, f32[320,128]{1,0:T(8,128)S(1)}, u32[]{:S(2)}, u32[]{:S(2)}) collective-permute-start(f32[320,128]{1,0:T(8,128)S(1)} %get-tuple-element.25), channel_id=1, source_target_pairs={{0,33},{33,0},{1,34},{34,1},{2,35},{35,2},{3,36},{36,3},{4,37},{37... | collective-permute-start | bytes 491528 | tf_op jit(solution)/shard_map/ppermute | solution.py:472
  37.4 2.2 %collective-permute-start.3 = (f32[320,128]{1,0:T(8,128)S(1)}, f32[320,128]{1,0:T(8,128)S(1)}, u32[]{:S(2)}, u32[]{:S(2)}) collective-permute-start(f32[320,128]{1,0:T(8,128)S(1)} %get-tuple-element.26), channel_id=1, source_target_pairs={{0,34},{34,0},{1,35},{35,1},{2,36},{36,2},{3,37},{37,3},{4,38},{38... | collective-permute-start | bytes 491528 | tf_op jit(solution)/shard_map/ppermute | solution.py:472
  39.6 0.0 copy-done.2
  39.6 0.5 basis.1
  40.2 0.2 collective-permute-done.2.one_in
  40.4 4.9 %collective-permute-done.3.two_in = f32[320,128]{1,0:T(8,128)S(1)} collective-permute-done((f32[320,128]{1,0:T(8,128)S(1)}, f32[320,128]{1,0:T(8,128)S(1)}, u32[]{:S(2)}, u32[]{:S(2)}) %collective-permute-start.3) | collective-permute-done | bytes 163872 | tf_op jit(solution)/shard_map/ppermute | solution.py:472
  45.3 0.0 copy-start.3
  45.3 0.0 copy-start.6
  45.3 0.0 copy-start.7
  45.3 5.0 %all-gather.2 = f32[112,128]{1,0:T(8,128)S(1)} all-gather(f32[56,128]{1,0:T(8,128)S(1)} %relay.1), channel_id=4, replica_groups={{32,3},{33,4},{34,5},{35,6},{36,7},{37,8},{38,9},{39,10},{40,11},{41,12..., dimensions={0}, use_global_device_ids=true | all-gather | bytes 86016 | tf_op jit(solution)/shard_map/all_gather | solution.py:575
  50.3 1.9 %all-gather.3 = f32[320,128]{1,0:T(8,128)S(1)} all-gather(f32[160,128]{1,0:T(8,128)S(1)} %exchange.1), channel_id=5, replica_groups={{0,32},{64,96},{128,160},{192,224},{256,288},{320,352},{384,416},{448,4..., dimensions={0}, use_global_device_ids=true | all-gather | bytes 245760 | tf_op jit(solution)/shard_map/all_gather | solution.py:586
  52.2 0.0 copy-done.3
  52.2 0.0 copy-done.6
  52.2 0.0 copy-done.7
  52.2 2.4 %potential.1 = f32[160,4,128]{2,1,0:T(4,128)} custom-call(f32[216,128]{1,0:T(8,128)S(1)} %get-tuple-element.24.kept.after, f32[320,128]{1,0:T(8,128)S(1)} %collective-permute-done.2.one_in, f32[320,128]{1,0:T(8,128)S(1)} %collective-permute-done.3.two_in, f32[2,160,128]{2,1,0:T(8,128)S(1)} %bitcast.22, s32[1,160]{1,0:T(1,128)S(1)} %bitcast.33, ...), custom_call_target="tpu_custom_call" | custom-call | flops 3000000000 | bytes 1000000 | tf_op jit(solution)/shard_map/potential/pallas_call | solution.py:588
  (4 shorter events, 0.1 us)
Async XLA Ops:
  2.9 12.5 %copy-start = (f32[96,25,25]{0,2,1:T(8,128)S(1)}, f32[96,25,25]{0,2,1:T(8,128)}, u32[]{:S(2)}) copy-start(f32[96,25,25]{0,2,1:T(8,128)} %param.16) | copy-start | bytes 720004
  2.9 12.5 %copy-start.1 = (f32[96,25,25]{0,2,1:T(8,128)S(1)}, f32[96,25,25]{0,2,1:T(8,128)}, u32[]{:S(2)}) copy-start(f32[96,25,25]{0,2,1:T(8,128)} %param.17) | copy-start | bytes 720004
  3.0 12.5 %copy-start.4 = (s32[96,3]{0,1:T(4,128)S(1)}, s32[96,3]{0,1:T(4,128)}, u32[]{:S(2)}) copy-start(s32[96,3]{0,1:T(4,128)} %param.14) | copy-start | bytes 3460
  3.0 12.5 %copy-start.5 = (s32[96,3]{0,1:T(4,128)S(1)}, s32[96,3]{0,1:T(4,128)}, u32[]{:S(2)}) copy-start(s32[96,3]{0,1:T(4,128)} %param.15) | copy-start | bytes 3460
  11.6 8.9 %collective-permute-start = (f32[264,128]{1,0:T(8,128)S(1)}, f32[264,128]{1,0:T(8,128)S(1)}, u32[]{:S(2)}, u32[]{:S(2)}) collective-permute-start(f32[264,128]{1,0:T(8,128)S(1)} %get-tuple-element.16.near), channel_id=1, source_target_pairs={{0,480},{32,64},{64,32},{96,128},{128,96},{160,192},{192,160},{224... | collective-permute-start | bytes 405512 | tf_op jit(solution)/shard_map/ppermute | solution.py:532
  13.5 7.0 %collective-permute-start.1 = (f32[56,128]{1,0:T(8,128)S(1)}, f32[56,128]{1,0:T(8,128)S(1)}, u32[]{:S(2)}, u32[]{:S(2)}) collective-permute-start(f32[56,128]{1,0:T(8,128)S(1)} %get-tuple-element.17), channel_id=1, source_target_pairs={{0,416},{32,128},{64,480},{96,192},{128,32},{160,256},{192,96},{22... | collective-permute-start | bytes 86024 | tf_op jit(solution)/shard_map/ppermute | solution.py:533
  24.7 15.0 %copy-start.2 = (f32[3,20480]{1,0:T(4,128)S(1)}, f32[3,20480]{1,0:T(4,128)}, u32[]{:S(2)}) copy-start(f32[3,20480]{1,0:T(4,128)} %param.10) | copy-start | bytes 737284
  26.1 14.2 %collective-permute-start.2 = (f32[320,128]{1,0:T(8,128)S(1)}, f32[320,128]{1,0:T(8,128)S(1)}, u32[]{:S(2)}, u32[]{:S(2)}) collective-permute-start(f32[320,128]{1,0:T(8,128)S(1)} %get-tuple-element.25), channel_id=1, source_target_pairs={{0,33},{33,0},{1,34},{34,1},{2,35},{35,2},{3,36},{36,3},{4,37},{37... | collective-permute-start | bytes 491528 | tf_op jit(solution)/shard_map/ppermute | solution.py:472
  37.4 7.8 %collective-permute-start.3 = (f32[320,128]{1,0:T(8,128)S(1)}, f32[320,128]{1,0:T(8,128)S(1)}, u32[]{:S(2)}, u32[]{:S(2)}) collective-permute-start(f32[320,128]{1,0:T(8,128)S(1)} %get-tuple-element.26), channel_id=1, source_target_pairs={{0,34},{34,0},{1,35},{35,1},{2,36},{36,2},{3,37},{37,3},{4,38},{38... | collective-permute-start | bytes 491528 | tf_op jit(solution)/shard_map/ppermute | solution.py:472
  45.3 7.0 %copy-start.3 = (f32[8,25,25]{2,0,1:T(8,128)S(1)}, f32[8,25,25]{2,0,1:T(8,128)}, u32[]{:S(2)}) copy-start(f32[8,25,25]{2,0,1:T(8,128)} %param.19) | copy-start | bytes 60004
  45.3 7.0 %copy-start.6 = (s32[160]{0:T(256)S(1)}, s32[160]{0:T(256)}, u32[]{:S(2)}) copy-start(s32[160]{0:T(256)} %param.12) | copy-start | bytes 1924
  45.3 7.0 %copy-start.7 = (s32[160]{0:T(256)S(1)}, s32[160]{0:T(256)}, u32[]{:S(2)}) copy-start(s32[160]{0:T(256)} %param.13) | copy-start | bytes 1924

commit v3 on v2

--- a/solution.py
+++ b/solution.py
@@ -150,10 +150,28 @@
     return jnp.concatenate([first < counts[:, :SLOT], second < counts[:, SLOT:]], axis=0)
 
 
+def row_sums(parts):
+    row = lax.broadcasted_iota(jnp.int32, parts[0].shape, 0)
+    upper = row < 4
+    parts = [
+        jnp.where(upper, a, b) + pltpu.roll(jnp.where(upper, b, a), 4, 0)
+        for a, b in zip(parts[:4], parts[4:])
+    ]
+    for distance in (2, 1):
+        here = (row // distance) % 2 == 0
+        half = len(parts) // 2
+        parts = [
+            jnp.where(here, a, b)
+            + jnp.where(here, pltpu.roll(a, 8 - distance, 0), pltpu.roll(b, distance, 0))
+            for a, b in zip(parts[:half], parts[half:])
+        ]
+    return parts[0]
+
+
 def moments_kernel(
     pos_in, charge_in, cell_in, count_in, upward_in, out, *scratch
 ):
-    pos, charge, cell, count, upward, basis, weight, sums, row, ops, done = scratch
+    pos, charge, cell, count, upward, basis, weight, row, ops, done = scratch
     copies = [
         pltpu.make_async_copy(source, target, done.at[n])
         for n, (source, target) in enumerate(
@@ -177,20 +195,23 @@
     live = live_t(count, row)
     for q in range(NQ):
         weight[q] = jnp.where(live, slots_down(charge[:, q, :]), 0.0)
-    sums[NQ * NP :, :] = jnp.zeros((LEAF - NQ * NP, LANES), F32)
-    for j in range(NP):
-        value = basis[j]
-        for q in range(NQ):
-            product = (weight[q] * value).reshape(BLKS // 8, 8, SLOT)
-            at = q * 24 + j if j < 24 else 96 + q
-            sums[at : at + 1, :SLOT] = jnp.sum(
-                jnp.sum(product[: SLOT // 8], axis=0), axis=0, keepdims=True
-            )
-            sums[at : at + 1, SLOT:] = jnp.sum(
-                jnp.sum(product[SLOT // 8 :], axis=0), axis=0, keepdims=True
-            )
+
+    def part(q, j):
+        terms = weight[q] if j == 0 else weight[q] * basis[j]
+        terms = terms.reshape(BLKS // 8, 8, SLOT)
+        return jnp.concatenate(
+            [jnp.sum(terms[: SLOT // 8], axis=0), jnp.sum(terms[SLOT // 8 :], axis=0)], axis=1
+        )
+
+    groups = [
+        row_sums([part(q, j) for j in range(start, start + 8)])
+        for q in range(NQ)
+        for start in range(0, 24, 8)
+    ]
+    zeros = jnp.zeros((8, LANES), F32)
+    groups.append(row_sums([part(q, 24) for q in range(NQ)] + [zeros] * 4))
     member = member_t(cell, row).T.astype(BF16)
-    high, low = split(sums[...])
+    high, low = split(jnp.concatenate(groups, axis=0))
     field = dot(high, member) + dot(low, member)
     out[0:LEAF, :] = field
     ops[...] = jnp.zeros_like(ops)
@@ -380,15 +401,17 @@
     )
 
 
-def basis_kernel(pos, after, basis):
+def basis_kernel(pos, cell, count, after, basis, live, member, row):
     del after
     coords = [slots_down(pos[:, d, :]) for d in range(3)]
     for j, value in enumerate(harmonics(*coords)):
         basis[j] = value
+    member[...] = member_t(cell, row).astype(BF16)
+    live[...] = live_t(count, row).astype(F32)
 
 
 def potential_kernel(
-    kept, one_in, two_in, last, cell, count, downward, basis, out, row, ops, spread, result
+    kept, one_in, two_in, last, downward, basis, live, member, out, ops, spread, result
 ):
     core = parity("gx")
     mine = pl.ds(pl.multiple_of(core * LEAF, 8), LEAF)
@@ -411,21 +434,19 @@
     local = jnp.concatenate(
         [unpacked(leaf, q, NQ) + pushed[:, q * NZ : (q + 1) * NZ] for q in range(NQ)], axis=0
     )
-    member = member_t(cell, row).astype(BF16)
     high, low = split(local)
-    spread[...] = dot(high, member) + dot(low, member)
-    live = live_t(count, row)
+    spread[...] = dot(high, member[...]) + dot(low, member[...])
     for start, size, lane in ((0, 64, 0), (64, 64, 0), (SLOT, EXTRA, SLOT)):
         totals = [None] * NQ
         for j in range(NP):
             value = basis[j, start : start + size, :]
             for q in range(NQ):
-                term = spread[q * PAD + j : q * PAD + j + 1, lane : lane + SLOT] * value
-                totals[q] = term if j == 0 else totals[q] + term
+                term = spread[q * PAD + j : q * PAD + j + 1, lane : lane + SLOT]
+                totals[q] = term if j == 0 else totals[q] + term * value
         for q in range(NQ):
             result[q, start : start + size, :] = totals[q]
     for q in range(NQ):
-        out[:, q, :] = blocks_down(jnp.where(live, result[q], 0.0))
+        out[:, q, :] = blocks_down(jnp.where(live[...] > 0.0, result[q], 0.0))
 
 
 def call(kernel, outs, scratch, specs, name, micros=1):
@@ -515,7 +536,6 @@
             pltpu.VMEM((NP, 8, NP), F32),
             pltpu.VMEM((NP, BLKS, SLOT), F32),
             pltpu.VMEM((NQ, BLKS, SLOT), F32),
-            pltpu.VMEM((LEAF, LANES), F32),
             index_row,
             pltpu.VMEM((2 * PAD, PAD), F32),
             pltpu.SemaphoreType.DMA((5,)),
@@ -573,13 +593,17 @@
     two = swap_y(two, 2)
     relayed = call(relay_kernel, [rows(PAIR)], [], [VMEM] * 3, "relay")(kept, one, two)
     three = lax.all_gather(relayed, ("gx", "gy"), axis_index_groups=column_pairs(3, 1))
-    basis = call(
+    basis, live, member = call(
         basis_kernel,
-        [jax.ShapeDtypeStruct((NP, BLKS, SLOT), F32)],
-        [],
-        [VMEM] * 2,
+        [
+            jax.ShapeDtypeStruct((NP, BLKS, SLOT), F32),
+            jax.ShapeDtypeStruct((BLKS, SLOT), F32),
+            jax.ShapeDtypeStruct((NZ, LANES), BF16),
+        ],
+        [index_row],
+        [VMEM] * 4,
         "basis",
-    )(pos, kept)
+    )(pos, cell, count, kept)
     passed = call(exchange_kernel, [rows(LEAF + PAIR)], [], [VMEM] * 4, "exchange")(
         kept, one, two, three
     )
@@ -589,7 +613,6 @@
         potential_kernel,
         [jax.ShapeDtypeStruct((BLKS, NQ, SLOT), F32)],
         [
-            index_row,
             pltpu.VMEM((PAD, 2 * PAD), F32),
             pltpu.VMEM((NQ * PAD, LANES), F32),
             pltpu.VMEM((NQ, BLKS, SLOT), F32),
@@ -597,7 +620,7 @@
         [VMEM] * 8,
         "potential",
         3,
-    )(kept, one, two, last, cell, count, downward, basis)
+    )(kept, one, two, last, downward, basis, live, member)
     return potential.transpose(1, 0, 2).reshape(NQ, BLKS * SLOT)
 
 

time: 54.9 us -> 54.6 us (level)
  no operation moved by 1% of the time
where the time goes in v3:
time: 54.6 us; the launch traced here: 54.4 us
  blocking collectives  19.6 us (36%)
  starting transfers between devices  17.3 us (32%)
  Pallas kernels  10.8 us (20%)
  waiting for transfers between devices  6.42 us (12%)
    ppermute x2, starting transfers between devices, swap_y(): return lax.ppermute(field, ('gx', 'gy'), route)  13.5 us
    all_gather x1, blocking collectives, per_device(): both = lax.all_gather(own_field, 'gx', axis_index_groups=chip_pairs())  8.58 us
    ppermute x2, waiting for transfers between devices, swap_y(): return lax.ppermute(field, ('gx', 'gy'), route)  5.03 us
    all_gather x1, blocking collectives, per_device(): lax.all_gather(relayed, ('gx', 'gy'), axis_index_groups=column_pairs(3, 1))  5 us
    all_gather x1, blocking collectives, per_device(): sides = lax.all_gather(side, 'gx', axis_index_groups=chip_pairs())  4.14 us
    pallas_call x1, Pallas kernels, per_device(): call(moments_kernel, [rows(LEAF + PAIR)], [pltpu.VMEM((BLKS, 3, SLOT), F3...  2.85 us
    pallas_call x1, Pallas kernels, per_device(): call(tables_kernel, [leaf_table, leaf_table, coarse_table, coarse_table],...  2.34 us
    pallas_call x1, Pallas kernels, per_device(): call(potential_kernel, [jax.ShapeDtypeStruct((BLKS, NQ, SLOT), F32)], [pl...  2.21 us
  transfers between devices with their start and end apart: 4, of which 3 were waited for; matrix products, arithmetic and copies ran while one was open for 0% of the time, Pallas kernels for 8%

profile of v3, /device:TPU:1, one launch (start us, length us, event | category | flops | bytes accessed | tf_op | source)
XLA Modules:
  0.0 54.4 jit_solution(1842567284839767928)
XLA Ops:
  0.0 2.9 %moments.1 = f32[160,128]{1,0:T(8,128)S(1)} custom-call(f32[160,3,128]{2,1,0:T(4,128)} %bitcast.27, f32[160,4,128]{2,1,0:T(4,128)} %bitcast.36, s32[1,160]{1,0:T(1,128)} %bitcast.32, s32[1,160]{1,0:T(1,128)} %bitcast.34, f32[25,8,25]{2,1,0:T(8,128)} %bitcast.37), custom_call_target="tpu_custom_call" | custom-call | flops 3000000000 | bytes 1000000 | tf_op jit(solution)/shard_map/moments/pallas_call | solution.py:528
  2.9 0.0 copy-start
  2.9 0.0 copy-start.1
  2.9 0.0 copy-start.4
  2.9 0.0 copy-start.5
  2.9 8.6 %all-gather = f32[320,128]{1,0:T(8,128)S(1)} all-gather(f32[160,128]{1,0:T(8,128)S(1)} %moments.1), channel_id=2, replica_groups={{0,32},{64,96},{128,160},{192,224},{256,288},{320,352},{384,416},{448,4..., dimensions={0}, use_global_device_ids=true | all-gather | bytes 245760 | tf_op jit(solution)/shard_map/all_gather | solution.py:548
  11.5 1.9 %collective-permute-start = (f32[264,128]{1,0:T(8,128)S(1)}, f32[264,128]{1,0:T(8,128)S(1)}, u32[]{:S(2)}, u32[]{:S(2)}) collective-permute-start(f32[264,128]{1,0:T(8,128)S(1)} %get-tuple-element.19.near), channel_id=1, source_target_pairs={{0,480},{32,64},{64,32},{96,128},{128,96},{160,192},{192,160},{224... | collective-permute-start | bytes 405512 | tf_op jit(solution)/shard_map/ppermute | solution.py:552
  13.4 1.9 %collective-permute-start.1 = (f32[56,128]{1,0:T(8,128)S(1)}, f32[56,128]{1,0:T(8,128)S(1)}, u32[]{:S(2)}, u32[]{:S(2)}) collective-permute-start(f32[56,128]{1,0:T(8,128)S(1)} %get-tuple-element.20), channel_id=1, source_target_pairs={{0,416},{32,128},{64,480},{96,192},{128,32},{160,256},{192,96},{22... | collective-permute-start | bytes 86024 | tf_op jit(solution)/shard_map/ppermute | solution.py:553
  15.4 0.0 copy-done
  15.4 0.0 copy-done.1
  15.4 0.0 copy-done.4
  15.4 0.0 copy-done.5
  15.4 2.3 %tables.1 = (bf16[384,896]{1,0:T(8,128)(2,1)S(1)}, bf16[384,896]{1,0:T(8,128)(2,1)S(1)}, bf16[320,896]{1,0:T(8,128)(2,1)S(1)}, bf16[320,896]{1,0:T(8,128)(2,1)S(1)}) custom-call(s32[3,96]{1,0:T(4,128)S(1)} %bitcast.30, s32[3,96]{1,0:T(4,128)S(1)} %bitcast.31, f32[25,25,96]{2,1,0:T(8,128)S(1)} %bitcast.25, f32[25,25,96]{2,1,0:T(8,128)S(1)} %bitcast.26), custom_call_target="tpu_custom_call" | custom-call | flops 2000000000 | bytes 1000000 | tf_op jit(solution)/shard_map/tables/pallas_call | solution.py:556
  17.7 1.3 %own.1 = (f32[192,512]{1,0:T(8,128)S(1)}, f32[160,256]{1,0:T(8,128)S(1)}) custom-call(f32[264,128]{1,0:T(8,128)S(1)} %get-tuple-element.19.near, bf16[384,896]{1,0:T(8,128)(2,1)S(1)} %get-tuple-element.23.leaf_k, bf16[320,896]{1,0:T(8,128)(2,1)S(1)} %get-tuple-element.24.coarse_k), custom_call_target="tpu_custom_call" | custom-call | flops 2000000000 | bytes 1000000 | tf_op jit(solution)/shard_map/own/pallas_call | solution.py:569
  19.0 1.4 %collective-permute-done.1.far = f32[56,128]{1,0:T(8,128)S(1)} collective-permute-done((f32[56,128]{1,0:T(8,128)S(1)}, f32[56,128]{1,0:T(8,128)S(1)}, u32[]{:S(2)}, u32[]{:S(2)}) %collective-permute-start.1) | collective-permute-done | bytes 28704 | tf_op jit(solution)/shard_map/ppermute | solution.py:553
  20.4 0.0 collective-permute-done.fields
  20.4 4.1 %all-gather.1 = f32[640,128]{1,0:T(8,128)S(1)} all-gather(f32[320,128]{1,0:T(8,128)S(1)} %join.1), channel_id=3, replica_groups={{0,32},{64,96},{128,160},{192,224},{256,288},{320,352},{384,416},{448,4..., dimensions={0}, use_global_device_ids=true | all-gather | bytes 491520 | tf_op jit(solution)/shard_map/all_gather | solution.py:581
  24.6 0.0 copy-start.2
  24.6 0.0 copy-start.6
  24.6 0.0 copy-start.7
  24.6 1.5 %translate.1 = (f32[320,128]{1,0:T(8,128)S(1)}, f32[320,128]{1,0:T(8,128)S(1)}, f32[216,128]{1,0:T(8,128)S(1)}) custom-call(f32[2,320,128]{2,1,0:T(8,128)S(1)} %bitcast.21, bf16[384,896]{1,0:T(8,128)(2,1)S(1)} %get-tuple-element.21.leaf_k, bf16[320,896]{1,0:T(8,128)(2,1)S(1)} %get-tuple-element.22.coarse_k, f32[192,512]{1,0:T(8,128)S(1)} %get-tuple-element.25.own_leaf, ...), custom_call_target="tpu_custom_call" | custom-call | flops 3000000000 | bytes 1000000 | tf_op jit(solution)/shard_map/translate/pallas_call | solution.py:583
  26.1 11.2 %collective-permute-start.2 = (f32[320,128]{1,0:T(8,128)S(1)}, f32[320,128]{1,0:T(8,128)S(1)}, u32[]{:S(2)}, u32[]{:S(2)}) collective-permute-start(f32[320,128]{1,0:T(8,128)S(1)} %get-tuple-element.28), channel_id=1, source_target_pairs={{0,33},{33,0},{1,34},{34,1},{2,35},{35,2},{3,36},{36,3},{4,37},{37... | collective-permute-start | bytes 491528 | tf_op jit(solution)/shard_map/ppermute | solution.py:493
  37.3 2.2 %collective-permute-start.3 = (f32[320,128]{1,0:T(8,128)S(1)}, f32[320,128]{1,0:T(8,128)S(1)}, u32[]{:S(2)}, u32[]{:S(2)}) collective-permute-start(f32[320,128]{1,0:T(8,128)S(1)} %get-tuple-element.29), channel_id=1, source_target_pairs={{0,34},{34,0},{1,35},{35,1},{2,36},{36,2},{3,37},{37,3},{4,38},{38... | collective-permute-start | bytes 491528 | tf_op jit(solution)/shard_map/ppermute | solution.py:493
  39.6 0.0 copy-done.2
  39.6 0.0 copy-done.6
  39.6 0.0 copy-done.7
  39.6 0.6 %basis.1 = (f32[25,160,128]{2,1,0:T(8,128)S(1)}, f32[160,128]{1,0:T(8,128)S(1)}, bf16[128,256]{1,0:T(8,128)(2,1)S(1)}) custom-call(f32[160,3,128]{2,1,0:T(4,128)S(1)} %bitcast.28, s32[1,160]{1,0:T(1,128)S(1)} %bitcast.33, s32[1,160]{1,0:T(1,128)S(1)} %bitcast.35, f32[216,128]{1,0:T(8,128)S(1)} %get-tuple-element.27.kept.after), custom_call_target="tpu_custom_call" | custom-call | flops 1000000000 | bytes 1000000 | tf_op jit(solution)/shard_map/basis/pallas_call | solution.py:596
  40.1 0.2 collective-permute-done.2.one_in
  40.3 4.9 %collective-permute-done.3.two_in = f32[320,128]{1,0:T(8,128)S(1)} collective-permute-done((f32[320,128]{1,0:T(8,128)S(1)}, f32[320,128]{1,0:T(8,128)S(1)}, u32[]{:S(2)}, u32[]{:S(2)}) %collective-permute-start.3) | collective-permute-done | bytes 163872 | tf_op jit(solution)/shard_map/ppermute | solution.py:493
  45.2 0.0 copy-start.3
  45.2 5.0 %all-gather.2 = f32[112,128]{1,0:T(8,128)S(1)} all-gather(f32[56,128]{1,0:T(8,128)S(1)} %relay.1), channel_id=4, replica_groups={{32,3},{33,4},{34,5},{35,6},{36,7},{37,8},{38,9},{39,10},{40,11},{41,12..., dimensions={0}, use_global_device_ids=true | all-gather | bytes 86016 | tf_op jit(solution)/shard_map/all_gather | solution.py:595
  50.2 1.9 %all-gather.3 = f32[320,128]{1,0:T(8,128)S(1)} all-gather(f32[160,128]{1,0:T(8,128)S(1)} %exchange.1), channel_id=5, replica_groups={{0,32},{64,96},{128,160},{192,224},{256,288},{320,352},{384,416},{448,4..., dimensions={0}, use_global_device_ids=true | all-gather | bytes 245760 | tf_op jit(solution)/shard_map/all_gather | solution.py:610
  52.1 0.0 copy-done.3
  52.1 2.2 %potential.1 = f32[160,4,128]{2,1,0:T(4,128)} custom-call(f32[216,128]{1,0:T(8,128)S(1)} %get-tuple-element.27.kept.after, f32[320,128]{1,0:T(8,128)S(1)} %collective-permute-done.2.one_in, f32[320,128]{1,0:T(8,128)S(1)} %collective-permute-done.3.two_in, f32[2,160,128]{2,1,0:T(8,128)S(1)} %bitcast.22, f32[25,8,25]{2,1,0:T(8,128)S(1)} %bitcast.29, ...), custom_call_target="tpu_custom_call" | custom-call | flops 3000000000 | bytes 1000000 | tf_op jit(solution)/shard_map/potential/pallas_call | solution.py:612
  (4 shorter events, 0.1 us)
Async XLA Ops:
  2.9 12.5 %copy-start = (f32[96,25,25]{0,2,1:T(8,128)S(1)}, f32[96,25,25]{0,2,1:T(8,128)}, u32[]{:S(2)}) copy-start(f32[96,25,25]{0,2,1:T(8,128)} %param.16) | copy-start | bytes 720004
  2.9 12.5 %copy-start.1 = (f32[96,25,25]{0,2,1:T(8,128)S(1)}, f32[96,25,25]{0,2,1:T(8,128)}, u32[]{:S(2)}) copy-start(f32[96,25,25]{0,2,1:T(8,128)} %param.17) | copy-start | bytes 720004
  2.9 12.5 %copy-start.4 = (s32[96,3]{0,1:T(4,128)S(1)}, s32[96,3]{0,1:T(4,128)}, u32[]{:S(2)}) copy-start(s32[96,3]{0,1:T(4,128)} %param.14) | copy-start | bytes 3460
  2.9 12.5 %copy-start.5 = (s32[96,3]{0,1:T(4,128)S(1)}, s32[96,3]{0,1:T(4,128)}, u32[]{:S(2)}) copy-start(s32[96,3]{0,1:T(4,128)} %param.15) | copy-start | bytes 3460
  11.5 8.9 %collective-permute-start = (f32[264,128]{1,0:T(8,128)S(1)}, f32[264,128]{1,0:T(8,128)S(1)}, u32[]{:S(2)}, u32[]{:S(2)}) collective-permute-start(f32[264,128]{1,0:T(8,128)S(1)} %get-tuple-element.19.near), channel_id=1, source_target_pairs={{0,480},{32,64},{64,32},{96,128},{128,96},{160,192},{192,160},{224... | collective-permute-start | bytes 405512 | tf_op jit(solution)/shard_map/ppermute | solution.py:552
  13.4 7.0 %collective-permute-start.1 = (f32[56,128]{1,0:T(8,128)S(1)}, f32[56,128]{1,0:T(8,128)S(1)}, u32[]{:S(2)}, u32[]{:S(2)}) collective-permute-start(f32[56,128]{1,0:T(8,128)S(1)} %get-tuple-element.20), channel_id=1, source_target_pairs={{0,416},{32,128},{64,480},{96,192},{128,32},{160,256},{192,96},{22... | collective-permute-start | bytes 86024 | tf_op jit(solution)/shard_map/ppermute | solution.py:553
  24.6 15.0 %copy-start.2 = (f32[3,20480]{1,0:T(4,128)S(1)}, f32[3,20480]{1,0:T(4,128)}, u32[]{:S(2)}) copy-start(f32[3,20480]{1,0:T(4,128)} %param.10) | copy-start | bytes 737284
  24.6 15.0 %copy-start.6 = (s32[160]{0:T(256)S(1)}, s32[160]{0:T(256)}, u32[]{:S(2)}) copy-start(s32[160]{0:T(256)} %param.12) | copy-start | bytes 1924
  24.6 15.0 %copy-start.7 = (s32[160]{0:T(256)S(1)}, s32[160]{0:T(256)}, u32[]{:S(2)}) copy-start(s32[160]{0:T(256)} %param.13) | copy-start | bytes 1924
  26.1 14.2 %collective-permute-start.2 = (f32[320,128]{1,0:T(8,128)S(1)}, f32[320,128]{1,0:T(8,128)S(1)}, u32[]{:S(2)}, u32[]{:S(2)}) collective-permute-start(f32[320,128]{1,0:T(8,128)S(1)} %get-tuple-element.28), channel_id=1, source_target_pairs={{0,33},{33,0},{1,34},{34,1},{2,35},{35,2},{3,36},{36,3},{4,37},{37... | collective-permute-start | bytes 491528 | tf_op jit(solution)/shard_map/ppermute | solution.py:493
  37.3 7.8 %collective-permute-start.3 = (f32[320,128]{1,0:T(8,128)S(1)}, f32[320,128]{1,0:T(8,128)S(1)}, u32[]{:S(2)}, u32[]{:S(2)}) collective-permute-start(f32[320,128]{1,0:T(8,128)S(1)} %get-tuple-element.29), channel_id=1, source_target_pairs={{0,34},{34,0},{1,35},{35,1},{2,36},{36,2},{3,37},{37,3},{4,38},{38... | collective-permute-start | bytes 491528 | tf_op jit(solution)/shard_map/ppermute | solution.py:493
  45.2 7.0 %copy-start.3 = (f32[8,25,25]{2,0,1:T(8,128)S(1)}, f32[8,25,25]{2,0,1:T(8,128)}, u32[]{:S(2)}) copy-start(f32[8,25,25]{2,0,1:T(8,128)} %param.19) | copy-start | bytes 60004

commit v4 on v3

--- a/solution.py
+++ b/solution.py
@@ -122,12 +122,6 @@
     extra = tile[SLOT:, :]
     runs = [extra[:, g * EXTRA : (g + 1) * EXTRA] for g in range(4)]
     return jnp.concatenate([tile[:SLOT, :].T, jnp.concatenate(runs, axis=0).T], axis=0)
-
-
-def blocks_down(tile):
-    extra = tile[SLOT:, :].T
-    runs = [extra[g * EXTRA : (g + 1) * EXTRA, :] for g in range(4)]
-    return jnp.concatenate([tile[:SLOT, :].T, jnp.concatenate(runs, axis=1)], axis=0)
 
 
 def spread_row(values, row):
@@ -411,8 +405,9 @@
 
 
 def potential_kernel(
-    kept, one_in, two_in, last, downward, basis, live, member, out, ops, spread, result
+    kept, one_in, two_in, last, downward, basis, live, member, out, *scratch
 ):
+    ops, spread, result, stage, done = scratch
     core = parity("gx")
     mine = pl.ds(pl.multiple_of(core * LEAF, 8), LEAF)
     leaf = kept[0:LEAF, :] + one_in[mine, :] + two_in[mine, :] + last[1 - core, 0:LEAF, :]
@@ -436,6 +431,10 @@
     )
     high, low = split(local)
     spread[...] = dot(high, member[...]) + dot(low, member[...])
+    copies = [
+        pltpu.make_async_copy(stage.at[0:SLOT], out.at[0:SLOT], done.at[0]),
+        pltpu.make_async_copy(stage.at[SLOT:BLKS], out.at[SLOT:BLKS], done.at[1]),
+    ]
     for start, size, lane in ((0, 64, 0), (64, 64, 0), (SLOT, EXTRA, SLOT)):
         totals = [None] * NQ
         for j in range(NP):
@@ -444,17 +443,28 @@
                 term = spread[q * PAD + j : q * PAD + j + 1, lane : lane + SLOT]
                 totals[q] = term if j == 0 else totals[q] + term * value
         for q in range(NQ):
-            result[q, start : start + size, :] = totals[q]
+            result[q, start : start + size, :] = jnp.where(
+                live[start : start + size, :] > 0.0, totals[q], 0.0
+            )
+        if start == 64:
+            for q in range(NQ):
+                stage[0:SLOT, q, :] = result[q, 0:SLOT, :].T
+            copies[0].start()
     for q in range(NQ):
-        out[:, q, :] = blocks_down(jnp.where(live[...] > 0.0, result[q], 0.0))
-
-
-def call(kernel, outs, scratch, specs, name, micros=1):
+        extra = result[q, SLOT:BLKS, :].T
+        runs = [extra[g * EXTRA : (g + 1) * EXTRA, :] for g in range(4)]
+        stage[SLOT:BLKS, q, :] = jnp.concatenate(runs, axis=1)
+    copies[1].start()
+    for copy in copies:
+        copy.wait()
+
+
+def call(kernel, outs, scratch, specs, name, micros=1, out_spec=VMEM):
     return pl.pallas_call(
         kernel,
         out_shape=outs if len(outs) > 1 else outs[0],
         in_specs=specs,
-        out_specs=[VMEM] * len(outs) if len(outs) > 1 else VMEM,
+        out_specs=[out_spec] * len(outs) if len(outs) > 1 else out_spec,
         scratch_shapes=scratch,
         cost_estimate=pl.CostEstimate(
             flops=int(micros * 1e9), bytes_accessed=1000000, transcendentals=0
@@ -616,10 +626,13 @@
             pltpu.VMEM((PAD, 2 * PAD), F32),
             pltpu.VMEM((NQ * PAD, LANES), F32),
             pltpu.VMEM((NQ, BLKS, SLOT), F32),
+            pltpu.VMEM((BLKS, NQ, SLOT), F32),
+            pltpu.SemaphoreType.DMA((2,)),
         ],
         [VMEM] * 8,
         "potential",
         3,
+        HBM,
     )(kept, one, two, last, downward, basis, live, member)
     return potential.transpose(1, 0, 2).reshape(NQ, BLKS * SLOT)
 

time: 54.6 us -> 54.5 us (level)
  no operation moved by 1% of the time
where the time goes in v4:
time: 54.5 us; the launch traced here: 54.3 us
  blocking collectives  19.6 us (36%)
  starting transfers between devices  17.3 us (32%)
  Pallas kernels  10.7 us (20%)
  waiting for transfers between devices  6.42 us (12%)
    ppermute x2, starting transfers between devices, swap_y(): return lax.ppermute(field, ('gx', 'gy'), route)  13.5 us
    all_gather x1, blocking collectives, per_device(): both = lax.all_gather(own_field, 'gx', axis_index_groups=chip_pairs())  8.58 us
    ppermute x2, waiting for transfers between devices, swap_y(): return lax.ppermute(field, ('gx', 'gy'), route)  5.03 us
    all_gather x1, blocking collectives, per_device(): lax.all_gather(relayed, ('gx', 'gy'), axis_index_groups=column_pairs(3, 1))  5 us
    all_gather x1, blocking collectives, per_device(): sides = lax.all_gather(side, 'gx', axis_index_groups=chip_pairs())  4.14 us
    pallas_call x1, Pallas kernels, per_device(): call(moments_kernel, [rows(LEAF + PAIR)], [pltpu.VMEM((BLKS, 3, SLOT), F3...  2.85 us
    pallas_call x1, Pallas kernels, per_device(): call(tables_kernel, [leaf_table, leaf_table, coarse_table, coarse_table],...  2.34 us
    pallas_call x1, Pallas kernels, per_device(): call(potential_kernel, [jax.ShapeDtypeStruct((BLKS, NQ, SLOT), F32)], [pl...  2.12 us
  transfers between devices with their start and end apart: 4, of which 3 were waited for; matrix products, arithmetic and copies ran while one was open for 0% of the time, Pallas kernels for 8%

profile of v4, /device:TPU:1, one launch (start us, length us, event | category | flops | bytes accessed | tf_op | source)
XLA Modules:
  0.0 54.3 jit_solution(17542342249132037317)
XLA Ops:
  0.0 2.9 %moments.1 = f32[160,128]{1,0:T(8,128)S(1)} custom-call(f32[160,3,128]{2,1,0:T(4,128)} %bitcast.27, f32[160,4,128]{2,1,0:T(4,128)} %bitcast.36, s32[1,160]{1,0:T(1,128)} %bitcast.32, s32[1,160]{1,0:T(1,128)} %bitcast.34, f32[25,8,25]{2,1,0:T(8,128)} %bitcast.37), custom_call_target="tpu_custom_call" | custom-call | flops 3000000000 | bytes 1000000 | tf_op jit(solution)/shard_map/moments/pallas_call | solution.py:538
  2.9 0.0 copy-start
  2.9 0.0 copy-start.1
  2.9 0.0 copy-start.4
  2.9 0.0 copy-start.5
  2.9 8.6 %all-gather = f32[320,128]{1,0:T(8,128)S(1)} all-gather(f32[160,128]{1,0:T(8,128)S(1)} %moments.1), channel_id=2, replica_groups={{0,32},{64,96},{128,160},{192,224},{256,288},{320,352},{384,416},{448,4..., dimensions={0}, use_global_device_ids=true | all-gather | bytes 245760 | tf_op jit(solution)/shard_map/all_gather | solution.py:558
  11.5 1.9 %collective-permute-start = (f32[264,128]{1,0:T(8,128)S(1)}, f32[264,128]{1,0:T(8,128)S(1)}, u32[]{:S(2)}, u32[]{:S(2)}) collective-permute-start(f32[264,128]{1,0:T(8,128)S(1)} %get-tuple-element.19.near), channel_id=1, source_target_pairs={{0,480},{32,64},{64,32},{96,128},{128,96},{160,192},{192,160},{224... | collective-permute-start | bytes 405512 | tf_op jit(solution)/shard_map/ppermute | solution.py:562
  13.4 1.9 %collective-permute-start.1 = (f32[56,128]{1,0:T(8,128)S(1)}, f32[56,128]{1,0:T(8,128)S(1)}, u32[]{:S(2)}, u32[]{:S(2)}) collective-permute-start(f32[56,128]{1,0:T(8,128)S(1)} %get-tuple-element.20), channel_id=1, source_target_pairs={{0,416},{32,128},{64,480},{96,192},{128,32},{160,256},{192,96},{22... | collective-permute-start | bytes 86024 | tf_op jit(solution)/shard_map/ppermute | solution.py:563
  15.4 0.0 copy-done
  15.4 0.0 copy-done.1
  15.4 0.0 copy-done.4
  15.4 0.0 copy-done.5
  15.4 2.3 %tables.1 = (bf16[384,896]{1,0:T(8,128)(2,1)S(1)}, bf16[384,896]{1,0:T(8,128)(2,1)S(1)}, bf16[320,896]{1,0:T(8,128)(2,1)S(1)}, bf16[320,896]{1,0:T(8,128)(2,1)S(1)}) custom-call(s32[3,96]{1,0:T(4,128)S(1)} %bitcast.30, s32[3,96]{1,0:T(4,128)S(1)} %bitcast.31, f32[25,25,96]{2,1,0:T(8,128)S(1)} %bitcast.25, f32[25,25,96]{2,1,0:T(8,128)S(1)} %bitcast.26), custom_call_target="tpu_custom_call" | custom-call | flops 2000000000 | bytes 1000000 | tf_op jit(solution)/shard_map/tables/pallas_call | solution.py:566
  17.7 1.3 %own.1 = (f32[192,512]{1,0:T(8,128)S(1)}, f32[160,256]{1,0:T(8,128)S(1)}) custom-call(f32[264,128]{1,0:T(8,128)S(1)} %get-tuple-element.19.near, bf16[384,896]{1,0:T(8,128)(2,1)S(1)} %get-tuple-element.23.leaf_k, bf16[320,896]{1,0:T(8,128)(2,1)S(1)} %get-tuple-element.24.coarse_k), custom_call_target="tpu_custom_call" | custom-call | flops 2000000000 | bytes 1000000 | tf_op jit(solution)/shard_map/own/pallas_call | solution.py:579
  19.0 1.4 %collective-permute-done.1.far = f32[56,128]{1,0:T(8,128)S(1)} collective-permute-done((f32[56,128]{1,0:T(8,128)S(1)}, f32[56,128]{1,0:T(8,128)S(1)}, u32[]{:S(2)}, u32[]{:S(2)}) %collective-permute-start.1) | collective-permute-done | bytes 28704 | tf_op jit(solution)/shard_map/ppermute | solution.py:563
  20.4 0.0 collective-permute-done.fields
  20.4 4.1 %all-gather.1 = f32[640,128]{1,0:T(8,128)S(1)} all-gather(f32[320,128]{1,0:T(8,128)S(1)} %join.1), channel_id=3, replica_groups={{0,32},{64,96},{128,160},{192,224},{256,288},{320,352},{384,416},{448,4..., dimensions={0}, use_global_device_ids=true | all-gather | bytes 491520 | tf_op jit(solution)/shard_map/all_gather | solution.py:591
  24.6 0.0 copy-start.2
  24.6 0.0 copy-start.6
  24.6 0.0 copy-start.7
  24.6 1.5 %translate.1 = (f32[320,128]{1,0:T(8,128)S(1)}, f32[320,128]{1,0:T(8,128)S(1)}, f32[216,128]{1,0:T(8,128)S(1)}) custom-call(f32[2,320,128]{2,1,0:T(8,128)S(1)} %bitcast.21, bf16[384,896]{1,0:T(8,128)(2,1)S(1)} %get-tuple-element.21.leaf_k, bf16[320,896]{1,0:T(8,128)(2,1)S(1)} %get-tuple-element.22.coarse_k, f32[192,512]{1,0:T(8,128)S(1)} %get-tuple-element.25.own_leaf, ...), custom_call_target="tpu_custom_call" | custom-call | flops 3000000000 | bytes 1000000 | tf_op jit(solution)/shard_map/translate/pallas_call | solution.py:593
  26.1 11.2 %collective-permute-start.2 = (f32[320,128]{1,0:T(8,128)S(1)}, f32[320,128]{1,0:T(8,128)S(1)}, u32[]{:S(2)}, u32[]{:S(2)}) collective-permute-start(f32[320,128]{1,0:T(8,128)S(1)} %get-tuple-element.28), channel_id=1, source_target_pairs={{0,33},{33,0},{1,34},{34,1},{2,35},{35,2},{3,36},{36,3},{4,37},{37... | collective-permute-start | bytes 491528 | tf_op jit(solution)/shard_map/ppermute | solution.py:503
  37.3 2.2 %collective-permute-start.3 = (f32[320,128]{1,0:T(8,128)S(1)}, f32[320,128]{1,0:T(8,128)S(1)}, u32[]{:S(2)}, u32[]{:S(2)}) collective-permute-start(f32[320,128]{1,0:T(8,128)S(1)} %get-tuple-element.29), channel_id=1, source_target_pairs={{0,34},{34,0},{1,35},{35,1},{2,36},{36,2},{3,37},{37,3},{4,38},{38... | collective-permute-start | bytes 491528 | tf_op jit(solution)/shard_map/ppermute | solution.py:503
  39.6 0.0 copy-done.2
  39.6 0.0 copy-done.6
  39.6 0.0 copy-done.7
  39.6 0.6 %basis.1 = (f32[25,160,128]{2,1,0:T(8,128)S(1)}, f32[160,128]{1,0:T(8,128)S(1)}, bf16[128,256]{1,0:T(8,128)(2,1)S(1)}) custom-call(f32[160,3,128]{2,1,0:T(4,128)S(1)} %bitcast.28, s32[1,160]{1,0:T(1,128)S(1)} %bitcast.33, s32[1,160]{1,0:T(1,128)S(1)} %bitcast.35, f32[216,128]{1,0:T(8,128)S(1)} %get-tuple-element.27.kept.after), custom_call_target="tpu_custom_call" | custom-call | flops 1000000000 | bytes 1000000 | tf_op jit(solution)/shard_map/basis/pallas_call | solution.py:606
  40.1 0.2 collective-permute-done.2.one_in
  40.3 4.9 %collective-permute-done.3.two_in = f32[320,128]{1,0:T(8,128)S(1)} collective-permute-done((f32[320,128]{1,0:T(8,128)S(1)}, f32[320,128]{1,0:T(8,128)S(1)}, u32[]{:S(2)}, u32[]{:S(2)}) %collective-permute-start.3) | collective-permute-done | bytes 163872 | tf_op jit(solution)/shard_map/ppermute | solution.py:503
  45.2 0.0 copy-start.3
  45.2 5.0 %all-gather.2 = f32[112,128]{1,0:T(8,128)S(1)} all-gather(f32[56,128]{1,0:T(8,128)S(1)} %relay.1), channel_id=4, replica_groups={{32,3},{33,4},{34,5},{35,6},{36,7},{37,8},{38,9},{39,10},{40,11},{41,12..., dimensions={0}, use_global_device_ids=true | all-gather | bytes 86016 | tf_op jit(solution)/shard_map/all_gather | solution.py:605
  50.2 1.9 %all-gather.3 = f32[320,128]{1,0:T(8,128)S(1)} all-gather(f32[160,128]{1,0:T(8,128)S(1)} %exchange.1), channel_id=5, replica_groups={{0,32},{64,96},{128,160},{192,224},{256,288},{320,352},{384,416},{448,4..., dimensions={0}, use_global_device_ids=true | all-gather | bytes 245760 | tf_op jit(solution)/shard_map/all_gather | solution.py:620
  52.1 0.0 copy-done.3
  52.1 2.1 %potential.1 = f32[160,4,128]{2,1,0:T(4,128)} custom-call(f32[216,128]{1,0:T(8,128)S(1)} %get-tuple-element.27.kept.after, f32[320,128]{1,0:T(8,128)S(1)} %collective-permute-done.2.one_in, f32[320,128]{1,0:T(8,128)S(1)} %collective-permute-done.3.two_in, f32[2,160,128]{2,1,0:T(8,128)S(1)} %bitcast.22, f32[25,8,25]{2,1,0:T(8,128)S(1)} %bitcast.29, ...), custom_call_target="tpu_custom_call" | custom-call | flops 3000000000 | bytes 1000000 | tf_op jit(solution)/shard_map/potential/pallas_call | solution.py:622
  (4 shorter events, 0.1 us)
Async XLA Ops:
  2.9 12.5 %copy-start = (f32[96,25,25]{0,2,1:T(8,128)S(1)}, f32[96,25,25]{0,2,1:T(8,128)}, u32[]{:S(2)}) copy-start(f32[96,25,25]{0,2,1:T(8,128)} %param.16) | copy-start | bytes 720004
  2.9 12.5 %copy-start.1 = (f32[96,25,25]{0,2,1:T(8,128)S(1)}, f32[96,25,25]{0,2,1:T(8,128)}, u32[]{:S(2)}) copy-start(f32[96,25,25]{0,2,1:T(8,128)} %param.17) | copy-start | bytes 720004
  2.9 12.5 %copy-start.4 = (s32[96,3]{0,1:T(4,128)S(1)}, s32[96,3]{0,1:T(4,128)}, u32[]{:S(2)}) copy-start(s32[96,3]{0,1:T(4,128)} %param.14) | copy-start | bytes 3460
  2.9 12.5 %copy-start.5 = (s32[96,3]{0,1:T(4,128)S(1)}, s32[96,3]{0,1:T(4,128)}, u32[]{:S(2)}) copy-start(s32[96,3]{0,1:T(4,128)} %param.15) | copy-start | bytes 3460
  11.5 8.9 %collective-permute-start = (f32[264,128]{1,0:T(8,128)S(1)}, f32[264,128]{1,0:T(8,128)S(1)}, u32[]{:S(2)}, u32[]{:S(2)}) collective-permute-start(f32[264,128]{1,0:T(8,128)S(1)} %get-tuple-element.19.near), channel_id=1, source_target_pairs={{0,480},{32,64},{64,32},{96,128},{128,96},{160,192},{192,160},{224... | collective-permute-start | bytes 405512 | tf_op jit(solution)/shard_map/ppermute | solution.py:562
  13.4 7.0 %collective-permute-start.1 = (f32[56,128]{1,0:T(8,128)S(1)}, f32[56,128]{1,0:T(8,128)S(1)}, u32[]{:S(2)}, u32[]{:S(2)}) collective-permute-start(f32[56,128]{1,0:T(8,128)S(1)} %get-tuple-element.20), channel_id=1, source_target_pairs={{0,416},{32,128},{64,480},{96,192},{128,32},{160,256},{192,96},{22... | collective-permute-start | bytes 86024 | tf_op jit(solution)/shard_map/ppermute | solution.py:563
  24.6 15.0 %copy-start.2 = (f32[3,20480]{1,0:T(4,128)S(1)}, f32[3,20480]{1,0:T(4,128)}, u32[]{:S(2)}) copy-start(f32[3,20480]{1,0:T(4,128)} %param.10) | copy-start | bytes 737284
  24.6 15.0 %copy-start.6 = (s32[160]{0:T(256)S(1)}, s32[160]{0:T(256)}, u32[]{:S(2)}) copy-start(s32[160]{0:T(256)} %param.12) | copy-start | bytes 1924
  24.6 15.0 %copy-start.7 = (s32[160]{0:T(256)S(1)}, s32[160]{0:T(256)}, u32[]{:S(2)}) copy-start(s32[160]{0:T(256)} %param.13) | copy-start | bytes 1924
  26.1 14.2 %collective-permute-start.2 = (f32[320,128]{1,0:T(8,128)S(1)}, f32[320,128]{1,0:T(8,128)S(1)}, u32[]{:S(2)}, u32[]{:S(2)}) collective-permute-start(f32[320,128]{1,0:T(8,128)S(1)} %get-tuple-element.28), channel_id=1, source_target_pairs={{0,33},{33,0},{1,34},{34,1},{2,35},{35,2},{3,36},{36,3},{4,37},{37... | collective-permute-start | bytes 491528 | tf_op jit(solution)/shard_map/ppermute | solution.py:503
  37.3 7.8 %collective-permute-start.3 = (f32[320,128]{1,0:T(8,128)S(1)}, f32[320,128]{1,0:T(8,128)S(1)}, u32[]{:S(2)}, u32[]{:S(2)}) collective-permute-start(f32[320,128]{1,0:T(8,128)S(1)} %get-tuple-element.29), channel_id=1, source_target_pairs={{0,34},{34,0},{1,35},{35,1},{2,36},{36,2},{3,37},{37,3},{4,38},{38... | collective-permute-start | bytes 491528 | tf_op jit(solution)/shard_map/ppermute | solution.py:503
  45.2 7.0 %copy-start.3 = (f32[8,25,25]{2,0,1:T(8,128)S(1)}, f32[8,25,25]{2,0,1:T(8,128)}, u32[]{:S(2)}) copy-start(f32[8,25,25]{2,0,1:T(8,128)} %param.19) | copy-start | bytes 60004

commit v5 on v4

--- a/solution.py
+++ b/solution.py
@@ -361,12 +361,12 @@
     for a in range(2):
         back(fields, a, sides[0, a * LEAF : (a + 1) * LEAF, :], 1)
         back(fields, 2 + a, sides[1, a * LEAF : (a + 1) * LEAF, :], 1)
+    spread(fields, [0, 1, 2, 3], high, low, 1)
+    result = product(leaf_k, high, low) + own_leaf[...]
+    blocks = [result[b * PAD : (b + 1) * PAD] for b in range(6)]
     spread(parents, [0, 1, 2, 3], coarse_high, coarse_low, 2)
-    spread(fields, [0, 1, 2, 3], high, low, 1)
     result = product(coarse_k, coarse_high, coarse_low) + own_coarse[...]
     coarse = [result[b * PAD : (b + 1) * PAD] for b in range(5)]
-    result = product(leaf_k, high, low) + own_leaf[...]
-    blocks = [result[b * PAD : (b + 1) * PAD] for b in range(6)]
     for t in range(2):
         emit(one_out, t * LEAF, blocks[3 * t + 1], NQ, LEAF)
         emit(two_out, t * LEAF, blocks[3 * t + 2], NQ, LEAF)

time: 54.5 us -> 54.6 us (level)
  no operation moved by 1% of the time
where the time goes in v5:
time: 54.6 us; the launch traced here: 54.3 us
  blocking collectives  19.6 us (36%)
  starting transfers between devices  17.3 us (32%)
  Pallas kernels  10.7 us (20%)
  waiting for transfers between devices  6.42 us (12%)
    ppermute x2, starting transfers between devices, swap_y(): return lax.ppermute(field, ('gx', 'gy'), route)  13.5 us
    all_gather x1, blocking collectives, per_device(): both = lax.all_gather(own_field, 'gx', axis_index_groups=chip_pairs())  8.58 us
    ppermute x2, waiting for transfers between devices, swap_y(): return lax.ppermute(field, ('gx', 'gy'), route)  5.03 us
    all_gather x1, blocking collectives, per_device(): lax.all_gather(relayed, ('gx', 'gy'), axis_index_groups=column_pairs(3, 1))  5 us
    all_gather x1, blocking collectives, per_device(): sides = lax.all_gather(side, 'gx', axis_index_groups=chip_pairs())  4.14 us
    pallas_call x1, Pallas kernels, per_device(): call(moments_kernel, [rows(LEAF + PAIR)], [pltpu.VMEM((BLKS, 3, SLOT), F3...  2.85 us
    pallas_call x1, Pallas kernels, per_device(): call(tables_kernel, [leaf_table, leaf_table, coarse_table, coarse_table],...  2.34 us
    pallas_call x1, Pallas kernels, per_device(): call(potential_kernel, [jax.ShapeDtypeStruct((BLKS, NQ, SLOT), F32)], [pl...  2.12 us
  transfers between devices with their start and end apart: 4, of which 3 were waited for; matrix products, arithmetic and copies ran while one was open for 0% of the time, Pallas kernels for 8%

profile of v5, /device:TPU:1, one launch (start us, length us, event | category | flops | bytes accessed | tf_op | source)
XLA Modules:
  0.0 54.3 jit_solution(5537492848891927332)
XLA Ops:
  0.0 2.9 %moments.1 = f32[160,128]{1,0:T(8,128)S(1)} custom-call(f32[160,3,128]{2,1,0:T(4,128)} %bitcast.27, f32[160,4,128]{2,1,0:T(4,128)} %bitcast.36, s32[1,160]{1,0:T(1,128)} %bitcast.32, s32[1,160]{1,0:T(1,128)} %bitcast.34, f32[25,8,25]{2,1,0:T(8,128)} %bitcast.37), custom_call_target="tpu_custom_call" | custom-call | flops 3000000000 | bytes 1000000 | tf_op jit(solution)/shard_map/moments/pallas_call | solution.py:538
  2.9 0.0 copy-start
  2.9 0.0 copy-start.1
  2.9 0.0 copy-start.4
  2.9 0.0 copy-start.5
  2.9 8.6 %all-gather = f32[320,128]{1,0:T(8,128)S(1)} all-gather(f32[160,128]{1,0:T(8,128)S(1)} %moments.1), channel_id=2, replica_groups={{0,32},{64,96},{128,160},{192,224},{256,288},{320,352},{384,416},{448,4..., dimensions={0}, use_global_device_ids=true | all-gather | bytes 245760 | tf_op jit(solution)/shard_map/all_gather | solution.py:558
  11.5 1.9 %collective-permute-start = (f32[264,128]{1,0:T(8,128)S(1)}, f32[264,128]{1,0:T(8,128)S(1)}, u32[]{:S(2)}, u32[]{:S(2)}) collective-permute-start(f32[264,128]{1,0:T(8,128)S(1)} %get-tuple-element.19.near), channel_id=1, source_target_pairs={{0,480},{32,64},{64,32},{96,128},{128,96},{160,192},{192,160},{224... | collective-permute-start | bytes 405512 | tf_op jit(solution)/shard_map/ppermute | solution.py:562
  13.4 1.9 %collective-permute-start.1 = (f32[56,128]{1,0:T(8,128)S(1)}, f32[56,128]{1,0:T(8,128)S(1)}, u32[]{:S(2)}, u32[]{:S(2)}) collective-permute-start(f32[56,128]{1,0:T(8,128)S(1)} %get-tuple-element.20), channel_id=1, source_target_pairs={{0,416},{32,128},{64,480},{96,192},{128,32},{160,256},{192,96},{22... | collective-permute-start | bytes 86024 | tf_op jit(solution)/shard_map/ppermute | solution.py:563
  15.4 0.0 copy-done
  15.4 0.0 copy-done.1
  15.4 0.0 copy-done.4
  15.4 0.0 copy-done.5
  15.4 2.3 %tables.1 = (bf16[384,896]{1,0:T(8,128)(2,1)S(1)}, bf16[384,896]{1,0:T(8,128)(2,1)S(1)}, bf16[320,896]{1,0:T(8,128)(2,1)S(1)}, bf16[320,896]{1,0:T(8,128)(2,1)S(1)}) custom-call(s32[3,96]{1,0:T(4,128)S(1)} %bitcast.30, s32[3,96]{1,0:T(4,128)S(1)} %bitcast.31, f32[25,25,96]{2,1,0:T(8,128)S(1)} %bitcast.25, f32[25,25,96]{2,1,0:T(8,128)S(1)} %bitcast.26), custom_call_target="tpu_custom_call" | custom-call | flops 2000000000 | bytes 1000000 | tf_op jit(solution)/shard_map/tables/pallas_call | solution.py:566
  17.7 1.3 %own.1 = (f32[192,512]{1,0:T(8,128)S(1)}, f32[160,256]{1,0:T(8,128)S(1)}) custom-call(f32[264,128]{1,0:T(8,128)S(1)} %get-tuple-element.19.near, bf16[384,896]{1,0:T(8,128)(2,1)S(1)} %get-tuple-element.23.leaf_k, bf16[320,896]{1,0:T(8,128)(2,1)S(1)} %get-tuple-element.24.coarse_k), custom_call_target="tpu_custom_call" | custom-call | flops 2000000000 | bytes 1000000 | tf_op jit(solution)/shard_map/own/pallas_call | solution.py:579
  19.0 1.4 %collective-permute-done.1.far = f32[56,128]{1,0:T(8,128)S(1)} collective-permute-done((f32[56,128]{1,0:T(8,128)S(1)}, f32[56,128]{1,0:T(8,128)S(1)}, u32[]{:S(2)}, u32[]{:S(2)}) %collective-permute-start.1) | collective-permute-done | bytes 28704 | tf_op jit(solution)/shard_map/ppermute | solution.py:563
  20.4 0.0 collective-permute-done.fields
  20.4 4.1 %all-gather.1 = f32[640,128]{1,0:T(8,128)S(1)} all-gather(f32[320,128]{1,0:T(8,128)S(1)} %join.1), channel_id=3, replica_groups={{0,32},{64,96},{128,160},{192,224},{256,288},{320,352},{384,416},{448,4..., dimensions={0}, use_global_device_ids=true | all-gather | bytes 491520 | tf_op jit(solution)/shard_map/all_gather | solution.py:591
  24.6 0.0 copy-start.2
  24.6 0.0 copy-start.6
  24.6 0.0 copy-start.7
  24.6 1.5 %translate.1 = (f32[320,128]{1,0:T(8,128)S(1)}, f32[320,128]{1,0:T(8,128)S(1)}, f32[216,128]{1,0:T(8,128)S(1)}) custom-call(f32[2,320,128]{2,1,0:T(8,128)S(1)} %bitcast.21, bf16[384,896]{1,0:T(8,128)(2,1)S(1)} %get-tuple-element.21.leaf_k, bf16[320,896]{1,0:T(8,128)(2,1)S(1)} %get-tuple-element.22.coarse_k, f32[192,512]{1,0:T(8,128)S(1)} %get-tuple-element.25.own_leaf, ...), custom_call_target="tpu_custom_call" | custom-call | flops 3000000000 | bytes 1000000 | tf_op jit(solution)/shard_map/translate/pallas_call | solution.py:593
  26.1 11.2 %collective-permute-start.2 = (f32[320,128]{1,0:T(8,128)S(1)}, f32[320,128]{1,0:T(8,128)S(1)}, u32[]{:S(2)}, u32[]{:S(2)}) collective-permute-start(f32[320,128]{1,0:T(8,128)S(1)} %get-tuple-element.28), channel_id=1, source_target_pairs={{0,33},{33,0},{1,34},{34,1},{2,35},{35,2},{3,36},{36,3},{4,37},{37... | collective-permute-start | bytes 491528 | tf_op jit(solution)/shard_map/ppermute | solution.py:503
  37.4 2.2 %collective-permute-start.3 = (f32[320,128]{1,0:T(8,128)S(1)}, f32[320,128]{1,0:T(8,128)S(1)}, u32[]{:S(2)}, u32[]{:S(2)}) collective-permute-start(f32[320,128]{1,0:T(8,128)S(1)} %get-tuple-element.29), channel_id=1, source_target_pairs={{0,34},{34,0},{1,35},{35,1},{2,36},{36,2},{3,37},{37,3},{4,38},{38... | collective-permute-start | bytes 491528 | tf_op jit(solution)/shard_map/ppermute | solution.py:503
  39.6 0.0 copy-done.2
  39.6 0.0 copy-done.6
  39.6 0.0 copy-done.7
  39.6 0.6 %basis.1 = (f32[25,160,128]{2,1,0:T(8,128)S(1)}, f32[160,128]{1,0:T(8,128)S(1)}, bf16[128,256]{1,0:T(8,128)(2,1)S(1)}) custom-call(f32[160,3,128]{2,1,0:T(4,128)S(1)} %bitcast.28, s32[1,160]{1,0:T(1,128)S(1)} %bitcast.33, s32[1,160]{1,0:T(1,128)S(1)} %bitcast.35, f32[216,128]{1,0:T(8,128)S(1)} %get-tuple-element.27.kept.after), custom_call_target="tpu_custom_call" | custom-call | flops 1000000000 | bytes 1000000 | tf_op jit(solution)/shard_map/basis/pallas_call | solution.py:606
  40.2 0.2 collective-permute-done.2.one_in
  40.3 4.9 %collective-permute-done.3.two_in = f32[320,128]{1,0:T(8,128)S(1)} collective-permute-done((f32[320,128]{1,0:T(8,128)S(1)}, f32[320,128]{1,0:T(8,128)S(1)}, u32[]{:S(2)}, u32[]{:S(2)}) %collective-permute-start.3) | collective-permute-done | bytes 163872 | tf_op jit(solution)/shard_map/ppermute | solution.py:503
  45.2 0.0 copy-start.3
  45.2 5.0 %all-gather.2 = f32[112,128]{1,0:T(8,128)S(1)} all-gather(f32[56,128]{1,0:T(8,128)S(1)} %relay.1), channel_id=4, replica_groups={{32,3},{33,4},{34,5},{35,6},{36,7},{37,8},{38,9},{39,10},{40,11},{41,12..., dimensions={0}, use_global_device_ids=true | all-gather | bytes 86016 | tf_op jit(solution)/shard_map/all_gather | solution.py:605
  50.2 1.9 %all-gather.3 = f32[320,128]{1,0:T(8,128)S(1)} all-gather(f32[160,128]{1,0:T(8,128)S(1)} %exchange.1), channel_id=5, replica_groups={{0,32},{64,96},{128,160},{192,224},{256,288},{320,352},{384,416},{448,4..., dimensions={0}, use_global_device_ids=true | all-gather | bytes 245760 | tf_op jit(solution)/shard_map/all_gather | solution.py:620
  52.2 0.0 copy-done.3
  52.2 2.1 %potential.1 = f32[160,4,128]{2,1,0:T(4,128)} custom-call(f32[216,128]{1,0:T(8,128)S(1)} %get-tuple-element.27.kept.after, f32[320,128]{1,0:T(8,128)S(1)} %collective-permute-done.2.one_in, f32[320,128]{1,0:T(8,128)S(1)} %collective-permute-done.3.two_in, f32[2,160,128]{2,1,0:T(8,128)S(1)} %bitcast.22, f32[25,8,25]{2,1,0:T(8,128)S(1)} %bitcast.29, ...), custom_call_target="tpu_custom_call" | custom-call | flops 3000000000 | bytes 1000000 | tf_op jit(solution)/shard_map/potential/pallas_call | solution.py:622
  (4 shorter events, 0.1 us)
Async XLA Ops:
  2.9 12.5 %copy-start = (f32[96,25,25]{0,2,1:T(8,128)S(1)}, f32[96,25,25]{0,2,1:T(8,128)}, u32[]{:S(2)}) copy-start(f32[96,25,25]{0,2,1:T(8,128)} %param.16) | copy-start | bytes 720004
  2.9 12.5 %copy-start.1 = (f32[96,25,25]{0,2,1:T(8,128)S(1)}, f32[96,25,25]{0,2,1:T(8,128)}, u32[]{:S(2)}) copy-start(f32[96,25,25]{0,2,1:T(8,128)} %param.17) | copy-start | bytes 720004
  2.9 12.5 %copy-start.4 = (s32[96,3]{0,1:T(4,128)S(1)}, s32[96,3]{0,1:T(4,128)}, u32[]{:S(2)}) copy-start(s32[96,3]{0,1:T(4,128)} %param.14) | copy-start | bytes 3460
  2.9 12.5 %copy-start.5 = (s32[96,3]{0,1:T(4,128)S(1)}, s32[96,3]{0,1:T(4,128)}, u32[]{:S(2)}) copy-start(s32[96,3]{0,1:T(4,128)} %param.15) | copy-start | bytes 3460
  11.5 8.9 %collective-permute-start = (f32[264,128]{1,0:T(8,128)S(1)}, f32[264,128]{1,0:T(8,128)S(1)}, u32[]{:S(2)}, u32[]{:S(2)}) collective-permute-start(f32[264,128]{1,0:T(8,128)S(1)} %get-tuple-element.19.near), channel_id=1, source_target_pairs={{0,480},{32,64},{64,32},{96,128},{128,96},{160,192},{192,160},{224... | collective-permute-start | bytes 405512 | tf_op jit(solution)/shard_map/ppermute | solution.py:562
  13.4 7.0 %collective-permute-start.1 = (f32[56,128]{1,0:T(8,128)S(1)}, f32[56,128]{1,0:T(8,128)S(1)}, u32[]{:S(2)}, u32[]{:S(2)}) collective-permute-start(f32[56,128]{1,0:T(8,128)S(1)} %get-tuple-element.20), channel_id=1, source_target_pairs={{0,416},{32,128},{64,480},{96,192},{128,32},{160,256},{192,96},{22... | collective-permute-start | bytes 86024 | tf_op jit(solution)/shard_map/ppermute | solution.py:563
  24.6 15.0 %copy-start.2 = (f32[3,20480]{1,0:T(4,128)S(1)}, f32[3,20480]{1,0:T(4,128)}, u32[]{:S(2)}) copy-start(f32[3,20480]{1,0:T(4,128)} %param.10) | copy-start | bytes 737284
  24.6 15.0 %copy-start.6 = (s32[160]{0:T(256)S(1)}, s32[160]{0:T(256)}, u32[]{:S(2)}) copy-start(s32[160]{0:T(256)} %param.12) | copy-start | bytes 1924
  24.6 15.0 %copy-start.7 = (s32[160]{0:T(256)S(1)}, s32[160]{0:T(256)}, u32[]{:S(2)}) copy-start(s32[160]{0:T(256)} %param.13) | copy-start | bytes 1924
  26.1 14.2 %collective-permute-start.2 = (f32[320,128]{1,0:T(8,128)S(1)}, f32[320,128]{1,0:T(8,128)S(1)}, u32[]{:S(2)}, u32[]{:S(2)}) collective-permute-start(f32[320,128]{1,0:T(8,128)S(1)} %get-tuple-element.28), channel_id=1, source_target_pairs={{0,33},{33,0},{1,34},{34,1},{2,35},{35,2},{3,36},{36,3},{4,37},{37... | collective-permute-start | bytes 491528 | tf_op jit(solution)/shard_map/ppermute | solution.py:503
  37.4 7.8 %collective-permute-start.3 = (f32[320,128]{1,0:T(8,128)S(1)}, f32[320,128]{1,0:T(8,128)S(1)}, u32[]{:S(2)}, u32[]{:S(2)}) collective-permute-start(f32[320,128]{1,0:T(8,128)S(1)} %get-tuple-element.29), channel_id=1, source_target_pairs={{0,34},{34,0},{1,35},{35,1},{2,36},{36,2},{3,37},{37,3},{4,38},{38... | collective-permute-start | bytes 491528 | tf_op jit(solution)/shard_map/ppermute | solution.py:503
  45.2 7.0 %copy-start.3 = (f32[8,25,25]{2,0,1:T(8,128)S(1)}, f32[8,25,25]{2,0,1:T(8,128)}, u32[]{:S(2)}) copy-start(f32[8,25,25]{2,0,1:T(8,128)} %param.19) | copy-start | bytes 60004
